TPU v7x, 256 devices: a whole 4x4x8 slice. The times are simulated.
256 devices in a mesh: gx: 8 (over z), gy: 32 (over y, x, core).
Axes of the slice: x: 4, y: 4, z: 8, core: 2. Of those that a mesh axis runs over, the one named last changes fastest.
Arguments:
- design_fraction: float32 [512, 256, 256], P('gx', 'gy'), may hold values from 0.05 to 1
- voltage_field: float32 [512, 256, 256], P('gx', 'gy'), may hold values from -6 to 6
- warmth_field: float32 [512, 256, 256], P('gx', 'gy'), may hold values from 0.5 to 2
- dual_state: float32 [512, 256, 256], P('gx', 'gy'), may hold values from -6 to 6
- injected_charge: float32 [512, 256, 256], P('gx', 'gy'), may hold values from -6 to 6
- objective_weighting: float32 [512, 256, 256], P('gx', 'gy'), may hold values from 0.1 to 1
- empty_flag: int32 [512, 256, 256], P('gx', 'gy'), may hold values 0 or 1
- solid_flag: int32 [512, 256, 256], P('gx', 'gy'), may hold values 0 or 1
- grounded_voltage_flag: int32 [512, 256, 256], P('gx', 'gy'), may hold values 0 or 1
- clamped_warmth_flag: int32 [512, 256, 256], P('gx', 'gy'), may hold values 0 or 1
Outputs:
- voltage_field_next: float32 [512, 256, 256], P('gx', 'gy')
- warmth_field_next: float32 [512, 256, 256], P('gx', 'gy')
- dual_state_next: float32 [512, 256, 256], P('gx', 'gy')
- scaled_derivative: float32 [512, 256, 256], P('gx', 'gy')
- occupied_fraction: float32 [], replicated
- mean_warmth: float32 [], replicated
All inputs are finite; a program needn't handle non-finite values. No bound on the sum of `empty_flag` or of `solid_flag` or of `grounded_voltage_flag` or of `clamped_warmth_flag` on one device may be relied on, other than what follows from the above.
Results may differ from a plain program's by a relative error of at most 0.00002.
Values sent between devices are 32-bit elements; how exact they have to be, the bound alone decides.
A program may use at most 64 MiB of HBM per device.

v0:
```python
import jax
import jax.numpy as jnp
from jax import lax
from jax.sharding import PartitionSpec as P

RADIUS = 3
WEIGHTS = (1.0, 2.0, 3.0, 4.0, 3.0, 2.0, 1.0)
CONDUCT_FLOOR = 0.001
CONDUCT_LOWEST = 0.05
DAMPING_FACTOR = 0.6
CORNERS = tuple(((a, b, c) for a in (0, 1) for b in (0, 1) for c in (0, 1)))


def extended_2(cells, sides, width):
    for axis, dim in sides:
        count = lax.axis_size(axis)
        ends = count - 1
        head = lax.slice_in_dim(cells, 0, width, axis=dim)
        tail = lax.slice_in_dim(cells, cells.shape[dim] - width, cells.shape[dim], axis=dim)
        cells = jnp.concatenate(
            [
                lax.ppermute(tail, axis, [(i, (i + 1) % count) for i in range(ends)]),
                cells,
                lax.ppermute(head, axis, [((i + 1) % count, i) for i in range(ends)]),
            ],
            axis=dim,
        )
    return cells


def shifted(shard, axis, by):
    peers = lax.axis_size(axis)
    pairs = [(i, i + by) for i in range(peers) if 0 <= i + by < peers]
    return lax.ppermute(shard, axis, pairs)


def tent_along(padded, direction, length):
    summed = WEIGHTS[0] * lax.slice_in_dim(padded, 0, length, axis=direction)
    for offset in range(1, 2 * RADIUS + 1):
        summed = summed + WEIGHTS[offset] * lax.slice_in_dim(
            padded, offset, offset + length, axis=direction
        )
    return summed


def window_sum(length, first_index, full_length):
    positions = first_index + jnp.arange(length, dtype=jnp.int32)
    summed = jnp.zeros((length,), jnp.float32)
    for offset in range(2 * RADIUS + 1):
        inside = (positions + offset - RADIUS >= 0) & (positions + offset - RADIUS < full_length)
        summed = summed + WEIGHTS[offset] * inside.astype(jnp.float32)
    return summed


def smooth(field):
    entry_dimensions = field.shape
    padded = extended_2(field, (("gx", 0),), RADIUS)
    along_x = tent_along(padded, 0, entry_dimensions[0])
    padded_y = extended_2(along_x, (("gy", 1),), RADIUS)
    along_y = tent_along(padded_y, 1, entry_dimensions[1])
    deeper = jnp.pad(along_y, ((0, 0), (0, 0), (RADIUS, RADIUS)))
    return tent_along(deeper, 2, entry_dimensions[2])


def vertex_pieces(extended, entry_dimensions):
    return [
        extended[
            a : a + entry_dimensions[0], b : b + entry_dimensions[1], c : c + entry_dimensions[2]
        ]
        for a, b, c in CORNERS
    ]


def element_apply(views, weight_field):
    overall = views[0]
    for corner in range(1, 8):
        overall = overall + views[corner]
    result = []
    for corner in range(8):
        nearby = views[corner ^ 4] + views[corner ^ 2] + views[corner ^ 1]
        result.append(weight_field * (5.0 / 12.0 * views[corner] + nearby / 12.0 - overall / 12.0))
    return result


def stored_work(left_views, right_views):
    images = element_apply(right_views, 1.0)
    summed = left_views[0] * images[0]
    for corner in range(1, 8):
        summed = summed + left_views[corner] * images[corner]
    return summed


def scatter_local(parts, entry_dimensions):
    extended = jnp.zeros(
        (entry_dimensions[0] + 1, entry_dimensions[1] + 1, entry_dimensions[2] + 1), jnp.float32
    )
    for corner, (a, b, c) in enumerate(CORNERS):
        extended = extended + jnp.pad(parts[corner], ((a, 1 - a), (b, 1 - b), (c, 1 - c)))
    return extended


def grow_higher(fields, from_y, from_x):
    rows_y = from_y(tuple((f[:, :1, :] for f in fields)))
    joined = [jnp.concatenate([f, r], axis=1) for f, r in zip(fields, rows_y)]
    rows_x = from_x(tuple((j[:1] for j in joined)))
    return [
        jnp.pad(jnp.concatenate([j, r], axis=0), ((0, 0), (0, 0), (0, 1)))
        for j, r in zip(joined, rows_x)
    ]


def fold_down(extended_list, to_x, to_y, entry_dimensions):
    trimmed = [e[:, :, : entry_dimensions[2]] for e in extended_list]
    arrived = to_x(tuple((t[entry_dimensions[0] :] for t in trimmed)))
    returned_onto = [t[: entry_dimensions[0]].at[0:1].add(r) for t, r in zip(trimmed, arrived)]
    arrived_y = to_y(tuple((f[:, entry_dimensions[1] :] for f in returned_onto)))
    return [f[:, : entry_dimensions[1]].at[:, 0:1].add(r) for f, r in zip(returned_onto, arrived_y)]


def per_device(
    design_fraction,
    voltage_field,
    warmth_field,
    dual_state,
    injected_charge,
    objective_weighting,
    empty_flag,
    solid_flag,
    grounded_voltage_flag,
    clamped_warmth_flag,
):
    entry_dimensions = design_fraction.shape
    count_x = lax.axis_size("gx")
    count_y = lax.axis_size("gy")
    start_x = lax.axis_index("gx") * entry_dimensions[0]
    start_y = lax.axis_index("gy") * entry_dimensions[1]
    full_x = entry_dimensions[0] * count_x
    full_y = entry_dimensions[1] * count_y
    element_number_sum = full_x * full_y * entry_dimensions[2]
    window = (
        window_sum(entry_dimensions[0], start_x, full_x)[:, None, None]
        * window_sum(entry_dimensions[1], start_y, full_y)[None, :, None]
        * window_sum(entry_dimensions[2], 0, entry_dimensions[2])[None, None, :]
    )
    electric_unfixed = 1.0 - grounded_voltage_flag.astype(jnp.float32)
    loose_warmth_flag = 1.0 - clamped_warmth_flag.astype(jnp.float32)
    solid = smooth(design_fraction) / window
    physical = jnp.where(empty_flag == 1, 0.0, jnp.where(solid_flag == 1, 1.0, solid))
    volume_local = jnp.sum(physical)
    occupied_fraction = lax.psum(volume_local, ("gx", "gy")) / element_number_sum
    cubed = physical * physical * physical
    elec_weight = CONDUCT_FLOOR + (1.0 - CONDUCT_FLOOR) * cubed
    conduction_factor = CONDUCT_LOWEST + (1.0 - CONDUCT_LOWEST) * cubed
    masked_values = [
        electric_unfixed * voltage_field,
        loose_warmth_flag * warmth_field,
        loose_warmth_flag * dual_state,
    ]
    diag_parts = [
        scatter_local([elec_weight / 3.0] * 8, entry_dimensions),
        scatter_local([conduction_factor / 3.0] * 8, entry_dimensions),
    ]
    diag_sums = fold_down(
        diag_parts, lambda v: shifted(v, "gx", 1), lambda v: shifted(v, "gy", 1), entry_dimensions
    )
    extended = grow_higher(
        masked_values, lambda v: shifted(v, "gy", -1), lambda v: shifted(v, "gx", -1)
    )
    weights_of = [elec_weight, conduction_factor, conduction_factor]
    images = [
        scatter_local(element_apply(vertex_pieces(e, entry_dimensions), w), entry_dimensions)
        for e, w in zip(extended, weights_of)
    ]
    returned_onto = fold_down(
        images, lambda v: shifted(v, "gx", 1), lambda v: shifted(v, "gy", 1), entry_dimensions
    )
    diag_e = electric_unfixed * diag_sums[0] + (1.0 - electric_unfixed)
    conduction_pivot = loose_warmth_flag * diag_sums[1] + (1.0 - loose_warmth_flag)
    applied_e = electric_unfixed * returned_onto[0] + (1.0 - electric_unfixed) * voltage_field
    conduction_product = (
        loose_warmth_flag * returned_onto[1] + (1.0 - loose_warmth_flag) * warmth_field
    )
    applied_a = loose_warmth_flag * returned_onto[2] + (1.0 - loose_warmth_flag) * dual_state
    voltage_field_next = (
        voltage_field + DAMPING_FACTOR * (electric_unfixed * injected_charge - applied_e) / diag_e
    )
    power_ext = grow_higher(
        [voltage_field_next], lambda v: shifted(v, "gy", -1), lambda v: shifted(v, "gx", -1)
    )[0]
    power_views = vertex_pieces(power_ext, entry_dimensions)
    resistive_power = stored_work(power_views, power_views)
    heat_ext = scatter_local([elec_weight * resistive_power / 8.0] * 8, entry_dimensions)
    warmth_injection = (
        loose_warmth_flag
        * fold_down(
            [heat_ext],
            lambda v: shifted(v, "gx", 1),
            lambda v: shifted(v, "gy", 1),
            entry_dimensions,
        )[0]
    )
    warmth_field_next = (
        warmth_field + DAMPING_FACTOR * (warmth_injection - conduction_product) / conduction_pivot
    )
    dual_state_next = (
        dual_state
        + DAMPING_FACTOR * (loose_warmth_flag * objective_weighting - applied_a) / conduction_pivot
    )
    element_warmth = jnp.sum(objective_weighting * warmth_field_next)
    mean_warmth = lax.psum(element_warmth, ("gx", "gy")) / element_number_sum
    solution_padded = grow_higher(
        [warmth_field_next, dual_state_next],
        lambda v: shifted(v, "gy", -1),
        lambda v: shifted(v, "gx", -1),
    )
    warmth_pieces = vertex_pieces(solution_padded[0], entry_dimensions)
    dual_windows = vertex_pieces(solution_padded[1], entry_dimensions)
    dual_average = dual_windows[0]
    for corner in range(1, 8):
        dual_average = dual_average + dual_windows[corner]
    dual_average = dual_average / 8.0
    derivative_part = 3.0 * physical * physical
    raw_derivative = derivative_part * (
        (1.0 - CONDUCT_FLOOR) * resistive_power * dual_average
        - (1.0 - CONDUCT_LOWEST) * stored_work(warmth_pieces, dual_windows)
    )
    design = (1.0 - empty_flag.astype(jnp.float32)) * (1.0 - solid_flag.astype(jnp.float32))
    filtered = smooth(raw_derivative * design / window)
    squares = lax.psum(jnp.sum(filtered * filtered), ("gx", "gy"))
    scale_norm = jnp.sqrt(squares / element_number_sum + 1e-06)
    scaled_derivative = filtered / scale_norm
    return (
        voltage_field_next,
        warmth_field_next,
        dual_state_next,
        scaled_derivative,
        occupied_fraction,
        mean_warmth,
    )


def solution(mesh):
    return jax.shard_map(
        per_device,
        mesh=mesh,
        in_specs=(
            P("gx", "gy", None),
            P("gx", "gy", None),
            P("gx", "gy", None),
            P("gx", "gy", None),
            P("gx", "gy", None),
            P("gx", "gy", None),
            P("gx", "gy", None),
            P("gx", "gy", None),
            P("gx", "gy", None),
            P("gx", "gy", None),
        ),
        out_specs=(
            P("gx", "gy", None),
            P("gx", "gy", None),
            P("gx", "gy", None),
            P("gx", "gy", None),
            P(),
            P(),
        ),
        check_vma=False,
    )
```

profile of v0, /device:TPU:2, one launch (start us, length us, event | category | flops | bytes accessed | tf_op | source)
XLA Modules:
  0.0 263.8 jit_solution(17859148522783031023)
XLA Ops:
  1.5 3.8 %collective-permute-start = (f32[3,8,256]{2,1,0:T(8,128)S(1)}, f32[3,8,256]{2,1,0:T(8,128)S(1)}, u32[]{:S(2)}, u32[]{:S(2)}) collective-permute-start(f32[3,8,256]{2,1,0:T(8,128)S(1)} %get-tuple-element.216), channel_id=1, source_target_pairs={{0,32},{32,64},{64,96},{96,128},{128,160},{160,192},{192,224},{1,3... | collective-permute-start | bytes 73736 | tf_op jit(solution)/shard_map/ppermute | solution.py:22
  10.2 2.5 collective-permute-start.14
  15.4 2.4 collective-permute-start.2
  17.8 3.2 %collective-permute-start.3 = (f32[64,3,256]{2,1,0:T(4,128)S(1)}, f32[64,3,256]{2,1,0:T(4,128)S(1)}, u32[]{:S(2)}, u32[]{:S(2)}) collective-permute-start(f32[64,3,256]{2,1,0:T(4,128)S(1)} %get-tuple-element.213), channel_id=1, source_target_pairs={{1,0},{2,1},{3,2},{4,3},{5,4},{6,5},{7,6},{8,7},{9,8},{10,9},{11,1... | collective-permute-start | bytes 589832 | tf_op jit(solution)/shard_map/ppermute | solution.py:24
  27.3 3.8 %collective-permute-done.21 = f32[1,9,256]{2,1,0:T(8,128)S(1)} collective-permute-done((f32[1,9,256]{2,1,0:T(8,128)S(1)}, f32[1,9,256]{2,1,0:T(8,128)S(1)}, u32[]{:S(2)}, u32[]{:S(2)}) %collective-permute-start.21) | collective-permute-done | bytes 9248 | tf_op jit(solution)/shard_map/ppermute | solution.py:34
  36.2 2.7 %subtract_multiply_fusion.2 = (f32[64,8,256]{2,1,0:T(8,128)S(1)}, f32[64,8,256]{2,1,0:T(8,128)S(1)}, f32[64,8,256]{2,1,0:T(8,128)S(1)}, f32[64,8,256]{2,1,0:T(8,...) fusion(f32[64,8,256]{2,1,0:T(8,128)S(1)} %get-tuple-element.160, ...), kind=kLoop, calls=%fused_computation.197 | loop fusion | flops 6291456 | bytes 11583488 | tf_op jit(solution)/shard_map/mul | solution.py:81
  41.7 4.1 %collective-permute-start.6 = (f32[1,9,256]{2,1,0:T(8,128)S(1)}, f32[1,9,256]{2,1,0:T(8,128)S(1)}, u32[]{:S(2)}, u32[]{:S(2)}) collective-permute-start(f32[1,9,256]{2,1,0:T(8,128)S(1)} %slice.907), channel_id=1, source_target_pairs={{0,32},{32,64},{64,96},{96,128},{128,160},{160,192},{192,224},{1,3... | collective-permute-start | bytes 27656 | tf_op jit(solution)/shard_map/ppermute | solution.py:34
  54.5 5.0 %collective-permute-start.16 = (f32[1,9,256]{2,1,0:T(8,128)S(1)}, f32[1,9,256]{2,1,0:T(8,128)S(1)}, u32[]{:S(2)}, u32[]{:S(2)}) collective-permute-start(f32[1,9,256]{2,1,0:T(8,128)S(1)} %slice.931), channel_id=1, source_target_pairs={{0,32},{32,64},{64,96},{96,128},{128,160},{160,192},{192,224},{1,3... | collective-permute-start | bytes 27656 | tf_op jit(solution)/shard_map/ppermute | solution.py:34
  59.5 5.1 %collective-permute-start.22 = (f32[1,9,256]{2,1,0:T(8,128)S(1)}, f32[1,9,256]{2,1,0:T(8,128)S(1)}, u32[]{:S(2)}, u32[]{:S(2)}) collective-permute-start(f32[1,9,256]{2,1,0:T(8,128)S(1)} %slice.946), channel_id=1, source_target_pairs={{0,32},{32,64},{64,96},{96,128},{128,160},{160,192},{192,224},{1,3... | collective-permute-start | bytes 27656 | tf_op jit(solution)/shard_map/ppermute | solution.py:34
  64.7 3.9 %collective-permute-start.18 = (f32[1,9,256]{2,1,0:T(8,128)S(1)}, f32[1,9,256]{2,1,0:T(8,128)S(1)}, u32[]{:S(2)}, u32[]{:S(2)}) collective-permute-start(f32[1,9,256]{2,1,0:T(8,128)S(1)} %slice.937), channel_id=1, source_target_pairs={{0,32},{32,64},{64,96},{96,128},{128,160},{160,192},{192,224},{1,3... | collective-permute-start | bytes 27656 | tf_op jit(solution)/shard_map/ppermute | solution.py:34
  68.6 3.9 %collective-permute-start.8 = (f32[1,9,256]{2,1,0:T(8,128)S(1)}, f32[1,9,256]{2,1,0:T(8,128)S(1)}, u32[]{:S(2)}, u32[]{:S(2)}) collective-permute-start(f32[1,9,256]{2,1,0:T(8,128)S(1)} %slice.913), channel_id=1, source_target_pairs={{0,32},{32,64},{64,96},{96,128},{128,160},{160,192},{192,224},{1,3... | collective-permute-start | bytes 27656 | tf_op jit(solution)/shard_map/ppermute | solution.py:34
  74.6 3.5 %collective-permute-start.9 = (f32[64,1,256]{2,1,0:T(1,128)S(1)}, f32[64,1,256]{2,1,0:T(1,128)S(1)}, u32[]{:S(2)}, u32[]{:S(2)}) collective-permute-start(f32[64,1,256]{2,1,0:T(1,128)S(1)} %slice.916), channel_id=1, source_target_pairs={{0,1},{1,2},{2,3},{3,4},{4,5},{5,6},{6,7},{7,8},{8,9},{9,10},{10,1... | collective-permute-start | bytes 196616 | tf_op jit(solution)/shard_map/ppermute | solution.py:34
  80.9 2.4 scatter-add.41
  96.3 3.2 %collective-permute-start.23 = (f32[64,1,256]{2,1,0:T(1,128)S(1)}, f32[64,1,256]{2,1,0:T(1,128)S(1)}, u32[]{:S(2)}, u32[]{:S(2)}) collective-permute-start(f32[64,1,256]{2,1,0:T(1,128)S(1)} %slice.949), channel_id=1, source_target_pairs={{0,1},{1,2},{2,3},{3,4},{4,5},{5,6},{6,7},{7,8},{8,9},{9,10},{10,1... | collective-permute-start | bytes 196616 | tf_op jit(solution)/shard_map/ppermute | solution.py:34
  103.4 4.0 %collective-permute-done.11 = f32[1,9,256]{2,1,0:T(8,128)S(1)} collective-permute-done((f32[1,9,256]{2,1,0:T(8,128)S(1)}, f32[1,9,256]{2,1,0:T(8,128)S(1)}, u32[]{:S(2)}, u32[]{:S(2)}) %collective-permute-start.11) | collective-permute-done | bytes 9248 | tf_op jit(solution)/shard_map/ppermute | solution.py:34
  111.2 3.9 %collective-permute-start.12 = (f32[1,9,256]{2,1,0:T(8,128)S(1)}, f32[1,9,256]{2,1,0:T(8,128)S(1)}, u32[]{:S(2)}, u32[]{:S(2)}) collective-permute-start(f32[1,9,256]{2,1,0:T(8,128)S(1)} %slice.922), channel_id=1, source_target_pairs={{0,32},{32,64},{64,96},{96,128},{128,160},{160,192},{192,224},{1,3... | collective-permute-start | bytes 27656 | tf_op jit(solution)/shard_map/ppermute | solution.py:34
  116.6 4.9 %collective-permute-start.13 = (f32[64,1,256]{2,1,0:T(1,128)S(1)}, f32[64,1,256]{2,1,0:T(1,128)S(1)}, u32[]{:S(2)}, u32[]{:S(2)}) collective-permute-start(f32[64,1,256]{2,1,0:T(1,128)S(1)} %slice.925), channel_id=1, source_target_pairs={{0,1},{1,2},{2,3},{3,4},{4,5},{5,6},{6,7},{7,8},{8,9},{9,10},{10,1... | collective-permute-start | bytes 196616 | tf_op jit(solution)/shard_map/ppermute | solution.py:34
  126.4 2.4 scatter-add.55
  132.1 2.7 %multiply_reduce_fusion = (f32[]{:T(128)}, f32[64,8,256]{2,1,0:T(8,128)S(1)}, f32[64,8,256]{2,1,0:T(8,128)S(1)}) fusion(f32[64,8,256]{2,1,0:T(8,128)} %param.39, f32[64,8,256]{2,1,0:T(8,128)} %param.36, f32[64,8,256]{2,1,0:T(8,128)S(1)} %copy-done.18, f32[64,8,256]{2,1,0:T(8,128)} %scatter-add.51, f32[64,8,256]{2,1,0:T(8,128)} %scatter-add.49, ...), kind=kLoop, calls=%fused_computation.180 | loop fusion | flops 3014655 | bytes 5242884 | tf_op jit(solution)/shard_map/reduce_sum | solution.py:209
  143.5 2.5 collective-permute-done.27
  150.5 3.9 %collective-permute-start.28 = (f32[3,8,256]{2,1,0:T(8,128)S(1)}, f32[3,8,256]{2,1,0:T(8,128)S(1)}, u32[]{:S(2)}, u32[]{:S(2)}) collective-permute-start(f32[3,8,256]{2,1,0:T(8,128)S(1)} %get-tuple-element.200), channel_id=1, source_target_pairs={{0,32},{32,64},{64,96},{96,128},{128,160},{160,192},{192,224},{1,3... | collective-permute-start | bytes 73736 | tf_op jit(solution)/shard_map/ppermute | solution.py:22
  155.9 4.2 %collective-permute-done.29 = f32[3,8,256]{2,1,0:T(8,128)S(1)} collective-permute-done((f32[3,8,256]{2,1,0:T(8,128)S(1)}, f32[3,8,256]{2,1,0:T(8,128)S(1)}, u32[]{:S(2)}, u32[]{:S(2)}) %collective-permute-start.29) | collective-permute-done | bytes 24608 | tf_op jit(solution)/shard_map/ppermute | solution.py:24
  162.7 3.3 %collective-permute-start.31 = (f32[64,3,256]{2,1,0:T(4,128)S(1)}, f32[64,3,256]{2,1,0:T(4,128)S(1)}, u32[]{:S(2)}, u32[]{:S(2)}) collective-permute-start(f32[64,3,256]{2,1,0:T(4,128)S(1)} %get-tuple-element.199), channel_id=1, source_target_pairs={{1,0},{2,1},{3,2},{4,3},{5,4},{6,5},{7,6},{8,7},{9,8},{10,9},{11,1... | collective-permute-start | bytes 589832 | tf_op jit(solution)/shard_map/ppermute | solution.py:24
  172.0 86.7 %all-reduce.56 = (f32[]{:T(128)}, f32[]{:T(128)}, f32[]{:T(128)}) all-reduce(f32[]{:T(128)} %get-tuple-element.157, f32[]{:T(128)} %get-tuple-element.155, f32[]{:T(128)} %get-tuple-element.153), channel_id=1, replica_groups=mesh['gx'=8,'gy'=32] {'gx','gy'}, use_global_device_ids=true, to_apply=%region_1.2 | all-reduce | flops 3 | bytes 24 | tf_op jit(solution)/shard_map/psum | solution.py:229
  (177 shorter events, 89.7 us)
Async XLA Ops:
  1.5 13.4 %collective-permute-start = (f32[3,8,256]{2,1,0:T(8,128)S(1)}, f32[3,8,256]{2,1,0:T(8,128)S(1)}, u32[]{:S(2)}, u32[]{:S(2)}) collective-permute-start(f32[3,8,256]{2,1,0:T(8,128)S(1)} %get-tuple-element.216), channel_id=1, source_target_pairs={{0,32},{32,64},{64,96},{96,128},{128,160},{160,192},{192,224},{1,3... | collective-permute-start | bytes 73736 | tf_op jit(solution)/shard_map/ppermute | solution.py:22
  5.4 9.7 %collective-permute-start.1 = (f32[3,8,256]{2,1,0:T(8,128)S(1)}, f32[3,8,256]{2,1,0:T(8,128)S(1)}, u32[]{:S(2)}, u32[]{:S(2)}) collective-permute-start(f32[3,8,256]{2,1,0:T(8,128)S(1)} %get-tuple-element.217), channel_id=1, source_target_pairs={{32,0},{64,32},{96,64},{128,96},{160,128},{192,160},{224,192},{33,... | collective-permute-start | bytes 73736 | tf_op jit(solution)/shard_map/ppermute | solution.py:24
  8.0 13.0 %collective-permute-start.4 = (f32[64,1,256]{2,1,0:T(1,128)S(1)}, f32[64,1,256]{2,1,0:T(1,128)S(1)}, u32[]{:S(2)}, u32[]{:S(2)}) collective-permute-start(f32[64,1,256]{2,1,0:T(1,128)S(1)} %slice.902), channel_id=1, source_target_pairs={{1,0},{2,1},{3,2},{4,3},{5,4},{6,5},{7,6},{8,7},{9,8},{10,9},{11,1... | collective-permute-start | bytes 196616 | tf_op jit(solution)/shard_map/ppermute | solution.py:34
  10.2 12.0 %collective-permute-start.14 = (f32[64,1,256]{2,1,0:T(1,128)S(1)}, f32[64,1,256]{2,1,0:T(1,128)S(1)}, u32[]{:S(2)}, u32[]{:S(2)}) collective-permute-start(f32[64,1,256]{2,1,0:T(1,128)S(1)} %slice.926), channel_id=1, source_target_pairs={{1,0},{2,1},{3,2},{4,3},{5,4},{6,5},{7,6},{8,7},{9,8},{10,9},{11,1... | collective-permute-start | bytes 196616 | tf_op jit(solution)/shard_map/ppermute | solution.py:34
  12.8 10.8 %collective-permute-start.20 = (f32[64,1,256]{2,1,0:T(1,128)S(1)}, f32[64,1,256]{2,1,0:T(1,128)S(1)}, u32[]{:S(2)}, u32[]{:S(2)}) collective-permute-start(f32[64,1,256]{2,1,0:T(1,128)S(1)} %slice.941), channel_id=1, source_target_pairs={{1,0},{2,1},{3,2},{4,3},{5,4},{6,5},{7,6},{8,7},{9,8},{10,9},{11,1... | collective-permute-start | bytes 196616 | tf_op jit(solution)/shard_map/ppermute | solution.py:34
  15.4 16.0 %collective-permute-start.2 = (f32[64,3,256]{2,1,0:T(4,128)S(1)}, f32[64,3,256]{2,1,0:T(4,128)S(1)}, u32[]{:S(2)}, u32[]{:S(2)}) collective-permute-start(f32[64,3,256]{2,1,0:T(4,128)S(1)} %get-tuple-element.212), channel_id=1, source_target_pairs={{0,1},{1,2},{2,3},{3,4},{4,5},{5,6},{6,7},{7,8},{8,9},{9,10},{10,1... | collective-permute-start | bytes 589832 | tf_op jit(solution)/shard_map/ppermute | solution.py:22
  17.8 13.6 %collective-permute-start.3 = (f32[64,3,256]{2,1,0:T(4,128)S(1)}, f32[64,3,256]{2,1,0:T(4,128)S(1)}, u32[]{:S(2)}, u32[]{:S(2)}) collective-permute-start(f32[64,3,256]{2,1,0:T(4,128)S(1)} %get-tuple-element.213), channel_id=1, source_target_pairs={{1,0},{2,1},{3,2},{4,3},{5,4},{6,5},{7,6},{8,7},{9,8},{10,9},{11,1... | collective-permute-start | bytes 589832 | tf_op jit(solution)/shard_map/ppermute | solution.py:24
  21.0 6.3 %collective-permute-start.5 = (f32[1,9,256]{2,1,0:T(8,128)S(1)}, f32[1,9,256]{2,1,0:T(8,128)S(1)}, u32[]{:S(2)}, u32[]{:S(2)}) collective-permute-start(f32[1,9,256]{2,1,0:T(8,128)S(1)} %pad_maximum_fusion.23), channel_id=1, source_target_pairs={{32,0},{64,32},{96,64},{128,96},{160,128},{192,160},{224,192},{33,... | collective-permute-start | bytes 27656 | tf_op jit(solution)/shard_map/ppermute | solution.py:34
  22.3 9.0 %collective-permute-start.15 = (f32[1,9,256]{2,1,0:T(8,128)S(1)}, f32[1,9,256]{2,1,0:T(8,128)S(1)}, u32[]{:S(2)}, u32[]{:S(2)}) collective-permute-start(f32[1,9,256]{2,1,0:T(8,128)S(1)} %pad_maximum_fusion.21), channel_id=1, source_target_pairs={{32,0},{64,32},{96,64},{128,96},{160,128},{192,160},{224,192},{33,... | collective-permute-start | bytes 27656 | tf_op jit(solution)/shard_map/ppermute | solution.py:34
  23.6 7.5 %collective-permute-start.21 = (f32[1,9,256]{2,1,0:T(8,128)S(1)}, f32[1,9,256]{2,1,0:T(8,128)S(1)}, u32[]{:S(2)}, u32[]{:S(2)}) collective-permute-start(f32[1,9,256]{2,1,0:T(8,128)S(1)} %pad_maximum_fusion.20), channel_id=1, source_target_pairs={{32,0},{64,32},{96,64},{128,96},{160,128},{192,160},{224,192},{33,... | collective-permute-start | bytes 27656 | tf_op jit(solution)/shard_map/ppermute | solution.py:34
  41.7 30.9 %collective-permute-start.6 = (f32[1,9,256]{2,1,0:T(8,128)S(1)}, f32[1,9,256]{2,1,0:T(8,128)S(1)}, u32[]{:S(2)}, u32[]{:S(2)}) collective-permute-start(f32[1,9,256]{2,1,0:T(8,128)S(1)} %slice.907), channel_id=1, source_target_pairs={{0,32},{32,64},{64,96},{96,128},{128,160},{160,192},{192,224},{1,3... | collective-permute-start | bytes 27656 | tf_op jit(solution)/shard_map/ppermute | solution.py:34
  54.5 23.6 %collective-permute-start.16 = (f32[1,9,256]{2,1,0:T(8,128)S(1)}, f32[1,9,256]{2,1,0:T(8,128)S(1)}, u32[]{:S(2)}, u32[]{:S(2)}) collective-permute-start(f32[1,9,256]{2,1,0:T(8,128)S(1)} %slice.931), channel_id=1, source_target_pairs={{0,32},{32,64},{64,96},{96,128},{128,160},{160,192},{192,224},{1,3... | collective-permute-start | bytes 27656 | tf_op jit(solution)/shard_map/ppermute | solution.py:34
  59.5 18.6 %collective-permute-start.22 = (f32[1,9,256]{2,1,0:T(8,128)S(1)}, f32[1,9,256]{2,1,0:T(8,128)S(1)}, u32[]{:S(2)}, u32[]{:S(2)}) collective-permute-start(f32[1,9,256]{2,1,0:T(8,128)S(1)} %slice.946), channel_id=1, source_target_pairs={{0,32},{32,64},{64,96},{96,128},{128,160},{160,192},{192,224},{1,3... | collective-permute-start | bytes 27656 | tf_op jit(solution)/shard_map/ppermute | solution.py:34
  64.7 26.1 %collective-permute-start.18 = (f32[1,9,256]{2,1,0:T(8,128)S(1)}, f32[1,9,256]{2,1,0:T(8,128)S(1)}, u32[]{:S(2)}, u32[]{:S(2)}) collective-permute-start(f32[1,9,256]{2,1,0:T(8,128)S(1)} %slice.937), channel_id=1, source_target_pairs={{0,32},{32,64},{64,96},{96,128},{128,160},{160,192},{192,224},{1,3... | collective-permute-start | bytes 27656 | tf_op jit(solution)/shard_map/ppermute | solution.py:34
  72.6 8.2 %collective-permute-start.7 = (f32[64,1,256]{2,1,0:T(1,128)S(1)}, f32[64,1,256]{2,1,0:T(1,128)S(1)}, u32[]{:S(2)}, u32[]{:S(2)}) collective-permute-start(f32[64,1,256]{2,1,0:T(1,128)S(1)} %slice.910), channel_id=1, source_target_pairs={{0,1},{1,2},{2,3},{3,4},{4,5},{5,6},{6,7},{7,8},{8,9},{9,10},{10,1... | collective-permute-start | bytes 196616 | tf_op jit(solution)/shard_map/ppermute | solution.py:34
  74.6 8.7 %collective-permute-start.9 = (f32[64,1,256]{2,1,0:T(1,128)S(1)}, f32[64,1,256]{2,1,0:T(1,128)S(1)}, u32[]{:S(2)}, u32[]{:S(2)}) collective-permute-start(f32[64,1,256]{2,1,0:T(1,128)S(1)} %slice.916), channel_id=1, source_target_pairs={{0,1},{1,2},{2,3},{3,4},{4,5},{5,6},{6,7},{7,8},{8,9},{9,10},{10,1... | collective-permute-start | bytes 196616 | tf_op jit(solution)/shard_map/ppermute | solution.py:34
  88.7 13.1 %collective-permute-start.10 = (f32[64,1,256]{2,1,0:T(1,128)S(1)}, f32[64,1,256]{2,1,0:T(1,128)S(1)}, u32[]{:S(2)}, u32[]{:S(2)}) collective-permute-start(f32[64,1,256]{2,1,0:T(1,128)S(1)} %slice.917), channel_id=1, source_target_pairs={{1,0},{2,1},{3,2},{4,3},{5,4},{6,5},{7,6},{8,7},{9,8},{10,9},{11,1... | collective-permute-start | bytes 196616 | tf_op jit(solution)/shard_map/ppermute | solution.py:34
  94.1 9.2 %collective-permute-start.17 = (f32[64,1,256]{2,1,0:T(1,128)S(1)}, f32[64,1,256]{2,1,0:T(1,128)S(1)}, u32[]{:S(2)}, u32[]{:S(2)}) collective-permute-start(f32[64,1,256]{2,1,0:T(1,128)S(1)} %slice.934), channel_id=1, source_target_pairs={{0,1},{1,2},{2,3},{3,4},{4,5},{5,6},{6,7},{7,8},{8,9},{9,10},{10,1... | collective-permute-start | bytes 196616 | tf_op jit(solution)/shard_map/ppermute | solution.py:34
  96.3 18.8 %collective-permute-start.23 = (f32[64,1,256]{2,1,0:T(1,128)S(1)}, f32[64,1,256]{2,1,0:T(1,128)S(1)}, u32[]{:S(2)}, u32[]{:S(2)}) collective-permute-start(f32[64,1,256]{2,1,0:T(1,128)S(1)} %slice.949), channel_id=1, source_target_pairs={{0,1},{1,2},{2,3},{3,4},{4,5},{5,6},{6,7},{7,8},{8,9},{9,10},{10,1... | collective-permute-start | bytes 196616 | tf_op jit(solution)/shard_map/ppermute | solution.py:34
  99.5 22.0 %collective-permute-start.19 = (f32[64,1,256]{2,1,0:T(1,128)S(1)}, f32[64,1,256]{2,1,0:T(1,128)S(1)}, u32[]{:S(2)}, u32[]{:S(2)}) collective-permute-start(f32[64,1,256]{2,1,0:T(1,128)S(1)} %slice.940), channel_id=1, source_target_pairs={{0,1},{1,2},{2,3},{3,4},{4,5},{5,6},{6,7},{7,8},{8,9},{9,10},{10,1... | collective-permute-start | bytes 196616 | tf_op jit(solution)/shard_map/ppermute | solution.py:34
  116.6 13.1 %collective-permute-start.13 = (f32[64,1,256]{2,1,0:T(1,128)S(1)}, f32[64,1,256]{2,1,0:T(1,128)S(1)}, u32[]{:S(2)}, u32[]{:S(2)}) collective-permute-start(f32[64,1,256]{2,1,0:T(1,128)S(1)} %slice.925), channel_id=1, source_target_pairs={{0,1},{1,2},{2,3},{3,4},{4,5},{5,6},{6,7},{7,8},{8,9},{9,10},{10,1... | collective-permute-start | bytes 196616 | tf_op jit(solution)/shard_map/ppermute | solution.py:34
  142.0 6.1 %collective-permute-start.25 = (f32[1,9,256]{2,1,0:T(8,128)S(1)}, f32[1,9,256]{2,1,0:T(8,128)S(1)}, u32[]{:S(2)}, u32[]{:S(2)}) collective-permute-start(f32[1,9,256]{2,1,0:T(8,128)S(1)} %pad_maximum_fusion.19), channel_id=1, source_target_pairs={{32,0},{64,32},{96,64},{128,96},{160,128},{192,160},{224,192},{33,... | collective-permute-start | bytes 27656 | tf_op jit(solution)/shard_map/ppermute | solution.py:34
  160.4 7.7 %collective-permute-start.30 = (f32[64,3,256]{2,1,0:T(4,128)S(1)}, f32[64,3,256]{2,1,0:T(4,128)S(1)}, u32[]{:S(2)}, u32[]{:S(2)}) collective-permute-start(f32[64,3,256]{2,1,0:T(4,128)S(1)} %get-tuple-element.198), channel_id=1, source_target_pairs={{0,1},{1,2},{2,3},{3,4},{4,5},{5,6},{6,7},{7,8},{8,9},{9,10},{10,1... | collective-permute-start | bytes 589832 | tf_op jit(solution)/shard_map/ppermute | solution.py:22
  162.7 7.2 %collective-permute-start.31 = (f32[64,3,256]{2,1,0:T(4,128)S(1)}, f32[64,3,256]{2,1,0:T(4,128)S(1)}, u32[]{:S(2)}, u32[]{:S(2)}) collective-permute-start(f32[64,3,256]{2,1,0:T(4,128)S(1)} %get-tuple-element.199), channel_id=1, source_target_pairs={{1,0},{2,1},{3,2},{4,3},{5,4},{6,5},{7,6},{8,7},{9,8},{10,9},{11,1... | collective-permute-start | bytes 589832 | tf_op jit(solution)/shard_map/ppermute | solution.py:24
  (28 other events, 221.1 us)
where the time goes:
time: 267 us; the launch traced here: 264 us
  blocking collectives  86.7 us (32%)
  starting transfers between devices  85.9 us (32%)
  other arithmetic  35.9 us (13%)
  waiting for transfers between devices  26.2 us (10%)
  local copies, waits for them, and re-layouts  23.1 us (9%)
  between operations  5.95 us (2%)
    psum x1, blocking collectives, per_device(): squares = lax.psum(jnp.sum(filtered * filtered), ('gx', 'gy'))  86.7 us
    ppermute x24, starting transfers between devices, shifted(): return lax.ppermute(shard, axis, pairs)  64.5 us
    ppermute x24, waiting for transfers between devices, shifted(): return lax.ppermute(shard, axis, pairs)  17.9 us
    scatter-add x6, local copies, waits for them, and re-layouts, fold_down(): f[:, :entry_dimensions[1]].at[:, 0:1].add(r)  14.3 us
    ppermute x4, starting transfers between devices, extended_2(): lax.ppermute(tail, axis, [(i, (i + 1) % count) for i in range(ends)])  12.3 us
    ppermute x4, starting transfers between devices, extended_2(): lax.ppermute(head, axis, [((i + 1) % count, i) for i in range(ends)])  9.05 us
    mul x6, other arithmetic, element_apply(): weight_field * (5.0 / 12.0 * views[corner] + nearby / 12.0 - overall / 12.0)  8.87 us
    add x6, other arithmetic, scatter_local(): extended + jnp.pad(parts[corner], ((a, 1 - a), (b, 1 - b), (c, 1 - c)))  8.04 us
  transfers between devices with their start and end apart: 32, of which 12 were waited for; matrix products, arithmetic and copies ran while one was open for 14% of the time, Pallas kernels for 0%

commit v1 on v0

v1 whole, which is shorter than its diff:
```python
import functools

import jax
import jax.numpy as jnp
from jax import lax
from jax.experimental import pallas as pl
from jax.experimental.pallas import tpu as pltpu
from jax.sharding import PartitionSpec as P

MESH = pl.DeviceIdType.MESH
F32 = jnp.float32
BF16 = jnp.bfloat16
PAD = 8
OFFSETS = ((0, 1), (0, -1), (1, 1), (-1, 1), (1, -1), (-1, -1), (1, 0), (-1, 0))


def lanes(shape):
    return lax.broadcasted_iota(jnp.int32, shape, len(shape) - 1)


def z_next(p):
    r = pltpu.roll(p, 127, axis=p.ndim - 1)
    lane = lanes(p.shape[1:])
    low = jnp.where(lane < 127, r[0], r[1])
    high = jnp.where(lane < 127, r[1], 0.0)
    return jnp.stack([low, high])


def z_prev(p):
    r = pltpu.roll(p, 1, axis=p.ndim - 1)
    lane = lanes(p.shape[1:])
    low = jnp.where(lane > 0, r[0], 0.0)
    high = jnp.where(lane > 0, r[1], r[0])
    return jnp.stack([low, high])


def rows_of(shape):
    return lax.broadcasted_iota(jnp.int32, shape, len(shape) - 2)


def y_next(p, row):
    r = pltpu.roll(p, 7, axis=1)
    return jnp.where(rows_of(p.shape) < 7, r, jnp.broadcast_to(row, p.shape))


def y_prev(p):
    r = pltpu.roll(p, 1, axis=1)
    return jnp.where(rows_of(p.shape) > 0, r, 0.0)


def yz_forward(p, row):
    q = y_next(p, row)
    s, d = p + q, q - p
    sz, dz = z_next(s), z_next(d)
    return s + sz, sz - s, d + dz, dz - d


def z_forward_rows(s, d):
    sz, dz = z_next(s), z_next(d)
    return s + sz, sz - s, d + dz, dz - d


def x_forward(a, b):
    return [a[i] + b[i] for i in range(1, 4)], [b[i] - a[i] for i in range(4)]


def weigh(sums, diffs, w):
    w1, w2, w3 = w * (1.0 / 48.0), w * (1.0 / 24.0), w * (1.0 / 16.0)
    return (
        [w3 * sums[0], w3 * sums[1], w2 * sums[2]],
        [w3 * diffs[0], w2 * diffs[1], w2 * diffs[2], w1 * diffs[3]],
    )


def x_backward(sums, diffs):
    front = [-diffs[0]] + [sums[i] - diffs[i + 1] for i in range(3)]
    behind = [diffs[0]] + [sums[i] + diffs[i + 1] for i in range(3)]
    return front, behind


def yz_backward(n):
    ns = (n[0] - n[2]) + y_prev(n[0] + n[2])
    nd = (n[1] - n[3]) + y_prev(n[1] + n[3])
    return (ns - nd) + z_prev(ns + nd)


def energy(sa, da, sb, db):
    three = da[0] * db[0] + sa[0] * sb[0] + sa[1] * sb[1]
    two = da[1] * db[1] + da[2] * db[2] + sa[2] * sb[2]
    return (1.0 / 16.0) * three + (1.0 / 24.0) * two + (1.0 / 48.0) * (da[3] * db[3])


def spread(p):
    t = p + y_prev(p)
    return t + z_prev(t)


def row_pack(ref, h, first, planes, row):
    every = ref.shape[1]
    flat = ref.reshape(2 * every * 8, 128)
    return flat[pl.ds((h * every + first) * 8 + row, planes, stride=8), :]


def row_add(ref, h, first, planes, row, value):
    every = ref.shape[1]
    flat = ref.reshape(2 * every * 8, 128)
    where = pl.ds((h * every + first) * 8 + row, planes, stride=8)
    flat[where, :] = flat[where, :] + value


def edge_column(edge, h, p):
    every = edge.shape[2]
    flat = edge.reshape(8 * 2 * every, 128)
    return flat[pl.ds(h * every + p, 8, stride=2 * every), :]


def kernel(
    nx, ny, n,
    des_in, v_in, t_in, d_in, q_in, o_in, e_in, s_in, g_in, c_in,
    v_out, t_out, d_out, f_out, occ_out, mean_out,
    des, raw, flg, fld, flx,
    cc, cup, cdn, flo, fhi, fup, fdn,
    wz, yf, ph, cub, cube, cubs, ca,
    kap, v1, v1lo, v1hi, v1up, v1dn,
    d1, d1hi, d1dn, t0, tr, t1, t1hi, t1dn, joule,
    sen, scc, sup, sdn, fil, slots1, slots2,
    in_sem, out_sem, send_sem, recv_sem, r1_send, r1_recv, r2_send, r2_recv,
):
    gx, gy = lax.axis_index("gx"), lax.axis_index("gy")
    group = min(16, ny)
    blocks = ny // group
    total = float(nx * n * ny * 8 * 256)
    end = PAD + n
    first_x, last_x = gx == 0, gx == nx - 1
    first_y, last_y = gy == 0, gy == ny - 1

    loads = []
    plan = [
        (des_in, lambda h: des.at[h, PAD:end]),
        (v_in, lambda h: raw.at[0, h]),
        (g_in, lambda h: flg.at[2, h]),
        (t_in, lambda h: raw.at[1, h]),
        (d_in, lambda h: raw.at[2, h]),
        (c_in, lambda h: flg.at[3, h]),
        (e_in, lambda h: flg.at[0, h]),
        (s_in, lambda h: flg.at[1, h]),
        (q_in, lambda h: raw.at[3, h]),
        (o_in, lambda h: raw.at[4, h]),
    ]
    for i, (src, dst) in enumerate(plan):
        pair = []
        for h in range(2):
            c = pltpu.make_async_copy(
                src.at[:, :, pl.ds(128 * h, 128)], dst(h), in_sem.at[2 * i + h]
            )
            c.start()
            pair.append(c)
        loads.append(pair)

    def loaded(*which):
        for i in which:
            for c in loads[i]:
                c.wait()

    barrier = pltpu.get_barrier_semaphore()

    def device(dx, dy):
        return (lax.rem(gx + (nx + dx), nx), lax.rem(gy + (ny + dy), ny))

    me1, block = lax.rem(gy, group), lax.div(gy, group)
    me2 = gx * blocks + block

    def peer1(k):
        return (gx, block * group + lax.rem(me1 + k, group))

    def peer2(k):
        other = lax.rem(me2 + k, nx * blocks)
        return (lax.div(other, blocks), lax.rem(other, blocks) * group + me1)

    for dx, dy in OFFSETS:
        pl.semaphore_signal(barrier, inc=1, device_id=device(dx, dy), device_id_type=MESH)
    for k in range(1, group):
        pl.semaphore_signal(barrier, inc=1, device_id=peer1(k), device_id_type=MESH)
    for k in range(1, nx * blocks):
        pl.semaphore_signal(barrier, inc=1, device_id=peer2(k), device_id_type=MESH)

    count = [0]

    def send(src, dst, dx, dy):
        k = count[0]
        count[0] += 1
        c = pltpu.make_async_remote_copy(
            src_ref=src, dst_ref=dst, send_sem=send_sem.at[k], recv_sem=recv_sem.at[k],
            device_id=device(dx, dy), device_id_type=MESH,
        )
        c.start()
        return c

    def send_up(src, dst):
        return [
            send(src, dst.at[:, :, PAD:end], 0, 1),
            send(src.at[:, :, n - PAD : n], dst.at[:, :, 0:PAD], 1, 1),
            send(src.at[:, :, 0:PAD], dst.at[:, :, end : end + PAD], -1, 1),
        ]

    def send_down(src, dst, both=True):
        some = [
            send(src, dst.at[:, :, PAD:end], 0, -1),
            send(src.at[:, :, 0:PAD], dst.at[:, :, end : end + PAD], -1, -1),
        ]
        if both:
            some.append(send(src.at[:, :, n - PAD : n], dst.at[:, :, 0:PAD], 1, -1))
        return some

    pending = []

    def arrived(copies):
        for c in copies:
            c.wait_recv()
        pending.extend(copies)

    def tails(ref, up, down):
        for h in range(2):
            r = [row_pack(ref, h, PAD, n, j) for j in (0, 1, 2, 5, 6, 7)]
            up[0, h] = r[3] + 2.0 * r[4] + 3.0 * r[5]
            up[1, h] = r[4] + 2.0 * r[5]
            up[2, h] = r[5]
            down[0, h] = r[0]
            down[1, h] = 2.0 * r[0] + r[1]
            down[2, h] = 3.0 * r[0] + 2.0 * r[1] + r[2]

    zero_rows = jnp.zeros((2, 2, end + PAD, 128), F32)
    cc[3:5] = zero_rows
    scc[3:5] = zero_rows
    wi = lax.broadcasted_iota(jnp.int32, (256, 256), 0)
    wj = lax.broadcasted_iota(jnp.int32, (256, 256), 1)
    wz[...] = jnp.maximum(4 - jnp.abs(wi - wj), 0).astype(F32).astype(BF16)

    loaded(0)
    tails(des, cup, cdn)
    pl.semaphore_wait(barrier, len(OFFSETS) + group - 1 + nx * blocks - 1)
    moving = send_up(cup, cc.at[0:3]) + send_down(cdn, cc.at[5:8])
    moving += [
        send(des.at[:, end - 4 : end], des.at[:, PAD - 4 : PAD], 1, 0),
        send(des.at[:, PAD : PAD + 3], des.at[:, end : end + 3], -1, 0),
    ]
    loaded(1, 2, 3, 4, 5, 6, 7)
    moving.append(send(flg.at[0:2, :, n - 1], flx, 1, 0))

    def mask_body(i, carry):
        x = i * 4
        free_e = flg[2, :, pl.ds(x, 4)] == 0
        free_t = flg[3, :, pl.ds(x, 4)] == 0
        fld[0, :, pl.ds(PAD + x, 4)] = jnp.where(free_e, raw[0, :, pl.ds(x, 4)], 0.0)
        fld[1, :, pl.ds(PAD + x, 4)] = jnp.where(free_t, raw[1, :, pl.ds(x, 4)], 0.0)
        fld[2, :, pl.ds(PAD + x, 4)] = jnp.where(free_t, raw[2, :, pl.ds(x, 4)], 0.0)
        return carry

    lax.fori_loop(0, n // 4, mask_body, 0)
    for f in range(3):
        for h in range(2):
            fup[f, h] = row_pack(fld.at[f], h, PAD, n, 7)
            fdn[f, h] = row_pack(fld.at[f], h, PAD, n, 0)
    fields_moving = send_up(fup, flo) + send_down(fdn, fhi)
    fields_moving += [
        send(fld.at[:, :, end - 1 : end], fld.at[:, :, PAD - 1 : PAD], 1, 0),
        send(fld.at[:, :, PAD : PAD + 1], fld.at[:, :, end : end + 1], -1, 0),
    ]

    row = lax.broadcasted_iota(jnp.int32, (8, 128), 0)

    def filter_y(ref, edge, p):
        for h in range(2):
            a = ref[h, p]
            out = 4.0 * a + edge_column(edge, h, p)
            for k in (1, 2, 3):
                out += jnp.where(row < 8 - k, float(4 - k), 0.0) * pltpu.roll(a, 8 - k, axis=0)
                out += jnp.where(row >= k, float(4 - k), 0.0) * pltpu.roll(a, k, axis=0)
            yf[h, p] = out

    def filter_y_all(ref, edge, low):
        def body(i, carry):
            for u in range(4):
                filter_y(ref, edge, PAD + 4 * i + u)
            return carry

        lax.fori_loop(0, n // 4, body, 0)
        for p in list(range(PAD - low, PAD)) + list(range(end, end + 3)):
            filter_y(ref, edge, p)

    def filter_xz(p, planes):
        halves = []
        for h in range(2):
            a = yf[h, pl.ds(p - 3, planes + 6)]
            a = a[:-1] + a[1:]
            a = a[:-2] + a[2:]
            a = a[:-1] + a[1:]
            a = a[:-2] + a[2:]
            halves.append(a.reshape(planes * 8, 128))
        a = jnp.concatenate(halves, axis=1)
        high = a.astype(BF16)
        rest = a - high.astype(F32)
        mid = rest.astype(BF16)
        low = (rest - mid.astype(F32)).astype(BF16)
        w = wz[...]
        out = (
            jnp.dot(low, w, preferred_element_type=F32)
            + jnp.dot(mid, w, preferred_element_type=F32)
            + jnp.dot(high, w, preferred_element_type=F32)
        )
        return jnp.stack(
            [out[:, :128].reshape(planes, 8, 128), out[:, 128:].reshape(planes, 8, 128)]
        )

    def inverse_window(i, full):
        w = jnp.where(i == 0, 10, jnp.where(i == 1, 13, jnp.where(i == 2, 15, 16)))
        k = full - 1 - i
        return jnp.where(k == 0, w - 6, jnp.where(k == 1, w - 3, jnp.where(k == 2, w - 1, w)))

    shape = (2, 8, 128)
    yy = gy * 8 + lax.broadcasted_iota(jnp.int32, shape, 1)
    zz = lax.broadcasted_iota(jnp.int32, shape, 0) * 128 + lax.broadcasted_iota(jnp.int32, shape, 2)
    inv_yz = 1.0 / (inverse_window(yy, ny * 8) * inverse_window(zz, 256)).astype(F32)
    touch_yz = (jnp.where(yy == 0, 1, 2) * jnp.where(zz == 0, 1, 2)).astype(F32)

    def inv_x(p):
        i = gx * n + (p - PAD)
        full = nx * n
        r = jnp.where(i == 0, 1 / 10.0, jnp.where(i == 1, 1 / 13.0, jnp.where(i == 2, 1 / 15.0, 1 / 16.0)))
        k = full - 1 - i
        return jnp.where(
            k == 0, 1 / 10.0, jnp.where(k == 1, 1 / 13.0, jnp.where(k == 2, 1 / 15.0, r))
        ).astype(F32)

    arrived(moving)

    def clear(edge, field, low, high):
        @pl.when(first_x)
        def _():
            if low:
                field[:, PAD - low : PAD] = jnp.zeros((2, low, 8, 128), F32)
            edge[:, :, 0:PAD] = jnp.zeros((8, 2, PAD, 128), F32)

        @pl.when(last_x)
        def _():
            field[:, end : end + high] = jnp.zeros((2, high, 8, 128), F32)
            edge[:, :, end : end + PAD] = jnp.zeros((8, 2, PAD, 128), F32)

        @pl.when(first_y)
        def _():
            edge[0:3] = jnp.zeros((3, 2, end + PAD, 128), F32)

        @pl.when(last_y)
        def _():
            edge[5:8] = jnp.zeros((3, 2, end + PAD, 128), F32)

    clear(cc, des, 4, 3)
    filter_y_all(des, cc, 4)
    there_x = jnp.where(first_x, 0.0, 1.0).astype(F32)
    there_y = jnp.where(first_y, 0.0, 1.0).astype(F32)

    def density(smoothed, p, e, s):
        solid = smoothed * inv_yz * inv_x(p)
        return jnp.where(e == 1, 0.0, jnp.where(s == 1, 1.0, solid))

    before = density(filter_xz(PAD - 2, 2)[:, 1], PAD - 1, flx[0], flx[1])
    cub[:, PAD - 1] = there_x * (before * before * before)

    def density_body(i, acc):
        p = PAD + 8 * i
        smoothed = filter_xz(p, 8)
        for u in range(8):
            x = 8 * i + u
            rho = density(smoothed[:, u], p + u, flg[0, :, x], flg[1, :, x])
            ph[:, x] = rho
            cub[:, p + u] = rho * rho * rho
            acc = acc + rho
        return acc

    occupied = lax.fori_loop(0, n // 8, density_body, jnp.zeros(shape, F32))

    for h in range(2):
        cubs[0, h] = row_pack(cub, h, 0, end, 7)
    cube_moving = [send(cubs, cube, 0, 1)]

    def gather_body(i, last):
        for u in range(4):
            now = spread(cub[:, PAD + 4 * i + u])
            ca[:, 4 * i + u] = now + last
            last = now
        return last

    lax.fori_loop(0, n // 4, gather_body, spread(cub[:, PAD - 1]))

    arrived(fields_moving)

    @pl.when(last_x)
    def _():
        fld[:, :, end] = jnp.zeros((3, 2, 8, 128), F32)
        flo[:, :, end : end + PAD] = jnp.zeros((3, 2, PAD, 128), F32)
        fhi[:, :, end : end + PAD] = jnp.zeros((3, 2, PAD, 128), F32)

    @pl.when(last_y)
    def _():
        fhi[...] = jnp.zeros((3, 2, end + PAD, 128), F32)

    weights = ((0.001, 0.999), (0.05, 0.95), (0.05, 0.95))

    def apply_main(f):
        base, slope = weights[f]

        def forward(p):
            return yz_forward(fld[f, :, p], fhi[f, :, pl.ds(p, 1)])

        def element(a, b, w):
            return x_backward(*weigh(*x_forward(a, b), w))

        a = forward(PAD - 1)
        b = forward(PAD)
        _, behind = element(a, b, there_x * base + slope * cub[:, PAD - 1])

        def body(i, carry):
            a, behind = carry
            for u in range(2):
                x = 2 * i + u
                b = forward(PAD + x + 1)
                front, new = element(a, b, base + slope * cub[:, PAD + x])
                kap[f, :, x] = yz_backward([front[c] + behind[c] for c in range(4)])
                a, behind = b, new
            return tuple(a), tuple(new)

        lax.fori_loop(0, n // 2, body, (tuple(b), tuple(behind)))

    def edge_weight(base, slope):
        where = lax.broadcasted_iota(jnp.int32, (2, end, 128), 1)
        real = jnp.where(where == PAD - 1, there_x, 1.0) * there_y
        return base * real + (slope * there_y) * cube[0]

    def apply_edge(f):
        low, own = flo[f, :, 0:end], fdn[f]
        mine = jnp.concatenate([fld_first(f, PAD - 8, 8), own], axis=1)
        s, d = mine + low, mine - low
        a = z_forward_rows(s, d)
        last_own = fld_first(f, end, 1)
        last_low = flo[f, :, end : end + 1]
        b_end = z_forward_rows(last_own + last_low, last_own - last_low)
        where = lax.broadcasted_iota(jnp.int32, (2, end, 128), 1)
        b = [
            jnp.where(where == end - 1, jnp.broadcast_to(b_end[c], a[c].shape), pltpu.roll(a[c], end - 1, axis=1))
            for c in range(4)
        ]
        front, behind = x_backward(*weigh(*x_forward(a, b), edge_weight(*weights[f])))
        m = [front[c] + pltpu.roll(behind[c], 1, axis=1) for c in range(4)]
        ns, nd = m[0] + m[2], m[1] + m[3]
        out = (ns - nd) + z_prev(ns + nd)
        for h in range(2):
            row_add(kap.at[f], h, 0, n, 0, out[h, PAD:end])

    def fld_first(f, p, planes):
        return jnp.stack([row_pack(fld.at[f], h, p, planes, 0) for h in range(2)])

    apply_main(0)

    arrived(cube_moving)
    apply_edge(0)
    edge_cube = cube[0] * there_y
    edge_cube = edge_cube + pltpu.roll(edge_cube, 1, axis=1)
    edge_cube = edge_cube + z_prev(edge_cube)
    for h in range(2):
        row_add(ca, h, 0, n, 0, edge_cube[h, PAD:end])

    def pivot(x, base, slope):
        cx = jnp.where(gx * n + x == 0, 1.0, 2.0).astype(F32)
        return base * (cx * touch_yz) + slope * ca[:, x]

    loaded(8, 9)

    def volt_body(i, carry):
        for u in range(4):
            x = 4 * i + u
            v = raw[0, :, x]
            moved = 1.8 * (raw[3, :, x] - kap[0, :, x]) / pivot(x, 0.001, 0.999)
            v1[:, PAD + x] = v + jnp.where(flg[2, :, x] == 0, moved, -0.6 * v)
        return carry

    lax.fori_loop(0, n // 4, volt_body, 0)
    for h in range(2):
        v1up[0, h] = row_pack(v1, h, PAD, n, 7)
        v1dn[0, h] = row_pack(v1, h, PAD, n, 0)
    volt_moving = send_up(v1up, v1lo) + send_down(v1dn, v1hi)
    volt_moving += [
        send(v1.at[:, end - 1 : end], v1.at[:, PAD - 1 : PAD], 1, 0),
        send(v1.at[:, PAD : PAD + 1], v1.at[:, end : end + 1], -1, 0),
    ]
    stores = []

    def store(src, dst):
        for h in range(2):
            c = pltpu.make_async_copy(
                src(h), dst.at[:, :, pl.ds(128 * h, 128)], out_sem.at[len(stores)]
            )
            c.start()
            stores.append(c)

    store(lambda h: v1.at[h, PAD:end], v_out)

    apply_main(2)
    apply_edge(2)
    apply_main(1)
    apply_edge(1)

    def heat_body(i, carry):
        for u in range(2):
            x = 2 * i + u
            free = flg[3, :, x] == 0
            step = 1.8 / pivot(x, 0.05, 0.95)
            d = raw[2, :, x]
            d1[:, PAD + x] = d + jnp.where(free, step * (raw[4, :, x] - kap[2, :, x]), -0.6 * d)
            t = raw[1, :, x]
            t0[:, x] = t - jnp.where(free, step * kap[1, :, x], 0.6 * t)
            tr[:, x] = jnp.where(free, step, 0.0)
        return carry

    lax.fori_loop(0, n // 2, heat_body, 0)
    for h in range(2):
        d1dn[0, h] = row_pack(d1, h, PAD, n, 0)
    dual_moving = send_down(d1dn, d1hi, both=False)
    dual_moving.append(send(d1.at[:, PAD : PAD + 1], d1.at[:, end : end + 1], -1, 0))
    store(lambda h: d1.at[h, PAD:end], d_out)

    arrived(volt_moving)

    def clear_high(field, *edges):
        @pl.when(last_x)
        def _():
            field[:, end] = jnp.zeros((2, 8, 128), F32)
            for edge in edges:
                edge[0, :, end : end + PAD] = jnp.zeros((2, PAD, 128), F32)

        @pl.when(last_y)
        def _():
            edges[0][0] = jnp.zeros((2, end + PAD, 128), F32)

    clear_high(v1, v1hi, v1lo)

    def volt_forward(p):
        return yz_forward(v1[:, p], v1hi[0, :, pl.ds(p, 1)])

    a = volt_forward(PAD - 1)
    b = volt_forward(PAD)
    s, d = x_forward(a, b)
    lead = energy(s, d, s, d) * ((there_x * 0.001 + 0.999 * cub[:, PAD - 1]) / 8.0)

    def joule_body(i, carry):
        a, last, acc = carry
        for u in range(2):
            x = 2 * i + u
            b = volt_forward(PAD + x + 1)
            s, d = x_forward(a, b)
            e = energy(s, d, s, d)
            joule[:, x] = e
            now = spread(e * (0.001 / 8.0 + (0.999 / 8.0) * cub[:, PAD + x]))
            t = t0[:, x] + tr[:, x] * (now + last)
            t1[:, PAD + x] = t
            acc = acc + raw[4, :, x] * t
            a, last = b, now
        return tuple(a), last, acc

    _, _, warm = lax.fori_loop(
        0, n // 2, joule_body, (tuple(b), spread(lead), jnp.zeros(shape, F32))
    )

    def edge_heat():
        low = v1lo[0, :, 0:end]
        own = jnp.stack([row_pack(v1, h, 0, end, 0) for h in range(2)])
        a = z_forward_rows(own + low, own - low)
        last_own = jnp.stack([row_pack(v1, h, end, 1, 0) for h in range(2)])
        last_low = v1lo[0, :, end : end + 1]
        b_end = z_forward_rows(last_own + last_low, last_own - last_low)
        where = lax.broadcasted_iota(jnp.int32, (2, end, 128), 1)
        b = [
            jnp.where(where == end - 1, jnp.broadcast_to(b_end[c], a[c].shape), pltpu.roll(a[c], end - 1, axis=1))
            for c in range(4)
        ]
        s, d = x_forward(a, b)
        e = energy(s, d, s, d) * (edge_weight(0.001, 0.999) * 0.125)
        e = e + pltpu.roll(e, 1, axis=1)
        return (e + z_prev(e))[:, PAD:end]

    extra = edge_heat()
    warm_rows = jnp.zeros((8, 128), F32)
    for h in range(2):
        more = extra[h] * row_pack(tr, h, 0, n, 0)
        row_add(t1, h, PAD, n, 0, more)
        warm_rows = warm_rows + jnp.sum(
            (more * row_pack(raw.at[4], h, 0, n, 0)).reshape(n // 8, 8, 128), axis=0
        )
        t1dn[0, h] = row_pack(t1, h, PAD, n, 0)
    temp_moving = send_down(t1dn, t1hi, both=False)
    temp_moving.append(send(t1.at[:, PAD : PAD + 1], t1.at[:, end : end + 1], -1, 0))
    store(lambda h: t1.at[h, PAD:end], t_out)

    arrived(dual_moving)
    arrived(temp_moving)
    clear_high(d1, d1hi)
    clear_high(t1, t1hi)

    def pair_forward(p):
        return (
            tuple(yz_forward(t1[:, p], t1hi[0, :, pl.ds(p, 1)])),
            tuple(yz_forward(d1[:, p], d1hi[0, :, pl.ds(p, 1)])),
        )

    def sens_body(i, carry):
        ta, da = carry
        for u in range(2):
            x = 2 * i + u
            tb, db = pair_forward(PAD + x + 1)
            ts, td = x_forward(ta, tb)
            ds, dd = x_forward(da, db)
            mean = (0.999 / 8.0) * (da[0] + db[0])
            rho = ph[:, x]
            raw_value = joule[:, x] * mean - 0.95 * energy(ts, td, ds, dd)
            value = (3.0 * rho * rho) * raw_value * inv_yz * inv_x(PAD + x)
            held = (flg[0, :, x] + flg[1, :, x]) == 0
            sen[:, PAD + x] = jnp.where(held, value, 0.0)
            ta, da = tb, db
        return ta, da

    lax.fori_loop(0, n // 2, sens_body, pair_forward(PAD))
    tails(sen, sup, sdn)
    sens_moving = send_up(sup, scc.at[0:3]) + send_down(sdn, scc.at[5:8])
    sens_moving += [
        send(sen.at[:, end - 3 : end], sen.at[:, PAD - 3 : PAD], 1, 0),
        send(sen.at[:, PAD : PAD + 3], sen.at[:, end : end + 3], -1, 0),
    ]
    arrived(sens_moving)
    clear(scc, sen, 3, 3)
    filter_y_all(sen, scc, 3)

    def last_body(i, acc):
        out = filter_xz(PAD + 8 * i, 8)
        fil[:, pl.ds(8 * i, 8)] = out
        return acc + jnp.sum(out * out, axis=1)

    square = lax.fori_loop(0, n // 8, last_body, jnp.zeros(shape, F32))

    def fold(a):
        return jnp.sum(a, axis=0, keepdims=True)

    message = jnp.concatenate(
        [
            fold(square[0] + square[1]),
            fold(occupied[0] + occupied[1]),
            fold(warm[0] + warm[1] + warm_rows),
            jnp.zeros((5, 128), F32),
        ],
        axis=0,
    )

    def exchange(value, slots, me, size, peer, sends, recvs):
        slots[me] = value
        out = []
        for k in range(1, size):
            c = pltpu.make_async_remote_copy(
                src_ref=slots.at[me], dst_ref=slots.at[me], send_sem=sends.at[k],
                recv_sem=recvs.at[me], device_id=peer(k), device_id_type=MESH,
            )
            c.start()
            out.append(c)
        for k in range(1, size):
            source = lax.rem(me + k, size)
            pltpu.make_async_remote_copy(
                src_ref=slots.at[source], dst_ref=slots.at[source], send_sem=sends.at[k],
                recv_sem=recvs.at[source], device_id=peer(k), device_id_type=MESH,
            ).wait_recv()
        for c in out:
            c.wait_send()
        result = slots[0]
        for k in range(1, size):
            result = result + slots[k]
        return result

    message = exchange(message, slots1, me1, group, peer1, r1_send, r1_recv)
    message = exchange(message, slots2, me2, nx * blocks, peer2, r2_send, r2_recv)
    sums = jnp.sum(message, axis=1, keepdims=True)
    scale = 1.0 / jnp.sqrt(sums[0:1] * (1.0 / total) + 1e-6)
    scale = jnp.broadcast_to(scale, (8, 128))

    def scale_body(i, carry):
        fil[:, pl.ds(8 * i, 8)] = fil[:, pl.ds(8 * i, 8)] * scale
        return carry

    lax.fori_loop(0, n // 8, scale_body, 0)
    store(lambda h: fil.at[h], f_out)
    occ_out[...] = jnp.broadcast_to(sums[1:2] * (1.0 / total), (8, 128))
    mean_out[...] = jnp.broadcast_to(sums[2:3] * (1.0 / total), (8, 128))
    for c in pending:
        c.wait_send()
    for c in stores:
        c.wait()


def per_device(nx, ny, *args):
    n = args[0].shape[0]
    assert args[0].shape[1:] == (8, 256) and n % 8 == 0
    field = jax.ShapeDtypeStruct(args[0].shape, F32)
    tile = jax.ShapeDtypeStruct((8, 128), F32)
    wide = n + 2 * PAD

    def vm(*shape, dtype=F32):
        return pltpu.VMEM(shape, dtype)

    planes = vm(2, wide, 8, 128)
    own = vm(2, n, 8, 128)
    edge = vm(1, 2, wide, 128)
    edge_out = vm(1, 2, n, 128)
    group = min(16, ny)
    second = nx * (ny // group)
    scratch = [
        planes, vm(5, 2, n, 8, 128), vm(4, 2, n, 8, 128, dtype=jnp.int32),
        vm(3, 2, wide, 8, 128), vm(2, 2, 8, 128, dtype=jnp.int32),
        vm(8, 2, wide, 128), vm(3, 2, n, 128), vm(3, 2, n, 128),
        vm(3, 2, wide, 128), vm(3, 2, wide, 128), vm(3, 2, n, 128), vm(3, 2, n, 128),
        vm(256, 256, dtype=BF16), planes, own, planes,
        vm(1, 2, PAD + n, 128), vm(1, 2, PAD + n, 128), own,
        vm(3, 2, n, 8, 128), planes, edge, edge, edge_out, edge_out,
        planes, edge, edge_out, own, own, planes, edge, edge_out, own,
        planes, vm(8, 2, wide, 128), vm(3, 2, n, 128), vm(3, 2, n, 128), own,
        vm(group, 8, 128), vm(second, 8, 128),
        pltpu.SemaphoreType.DMA((20,)), pltpu.SemaphoreType.DMA((8,)),
        pltpu.SemaphoreType.DMA((48,)), pltpu.SemaphoreType.DMA((48,)),
        pltpu.SemaphoreType.DMA((group,)), pltpu.SemaphoreType.DMA((group,)),
        pltpu.SemaphoreType.DMA((second,)), pltpu.SemaphoreType.DMA((second,)),
    ]
    anywhere = pl.BlockSpec(memory_space=pl.ANY)
    vmem = pl.BlockSpec(memory_space=pltpu.VMEM)
    out = pl.pallas_call(
        functools.partial(kernel, nx, ny, n),
        out_shape=(field, field, field, field, tile, tile),
        in_specs=[anywhere] * 10,
        out_specs=(anywhere,) * 4 + (vmem, vmem),
        scratch_shapes=scratch,
        compiler_params=pltpu.CompilerParams(
            collective_id=0, has_side_effects=True, vmem_limit_bytes=56 * 1024 * 1024
        ),
    )(*args)
    return out[:4] + (out[4][0, 0], out[5][0, 0])


def solution(mesh):
    spec = P("gx", "gy", None)
    return jax.shard_map(
        functools.partial(per_device, mesh.shape["gx"], mesh.shape["gy"]),
        mesh=mesh,
        in_specs=(spec,) * 10,
        out_specs=(spec,) * 4 + (P(), P()),
        check_vma=False,
    )
```

time: 267 us -> 81.3 us (0.30)
  blocking collectives: 86.7 us -> 0 us
  starting transfers between devices: 85.9 us -> 0 us
  Pallas kernels: 0 us -> 71.8 us
  other arithmetic: 35.9 us -> 0 us
  waiting for transfers between devices: 26.2 us -> 0 us
  local copies, waits for them, and re-layouts: 23.1 us -> 7.56 us
  between operations: 5.95 us -> 0.65 us
    psum x1 -> x0, blocking collectives: 86.7 us -> none  [per_device(): squares = lax.psum(jnp.sum(filtered * filtered), ('gx', 'gy'))]
    ppermute x32 -> x0, starting transfers between devices: 85.9 us -> none  [the longest x24 64.5 us: shifted(): return lax.ppermute(shard, axis, pairs)]
    pallas_call x0 -> x1, Pallas kernels: none -> 71.8 us  [per_device(): pl.pallas_call(functools.partial(kernel, nx, ny, n), out_shape=(field, fi...]
    ppermute x32 -> x0, waiting for transfers between devices: 26.2 us -> none  [the longest x24 17.9 us: shifted(): return lax.ppermute(shard, axis, pairs)]
    scatter-add x6 -> x0, local copies, waits for them, and re-layouts: 14.3 us -> none  [fold_down(): f[:, :entry_dimensions[1]].at[:, 0:1].add(r)]
    add x20 -> x0, other arithmetic: 13.2 us -> none  [the longest x6 8.04 us: scatter_local(): extended + jnp.pad(parts[corner], ((a, 1 - a), (b, 1 - b), (c, 1 - c)))]
    mul x9 -> x0, other arithmetic: 10.3 us -> none  [the longest x6 8.87 us: element_apply(): weight_field * (5.0 / 12.0 * views[corner] + nearby / 12.0 - overall / 12.0)]
    reduce_sum x3 -> x0, other arithmetic: 5.76 us -> none  [the longest x1 2.73 us: per_device(): element_warmth = jnp.sum(objective_weighting * warmth_field_next)]
  transfers between devices with their start and end apart: 32 -> 0, of which waited for: 12 -> 0; matrix products, arithmetic and copies ran while one was open for 14% -> 0% of each run, Pallas kernels for 0% -> 0%
where the time goes in v1:
time: 81.3 us; the launch traced here: 80 us
  Pallas kernels  71.8 us (88%)
  local copies, waits for them, and re-layouts  7.56 us (9%)
    pallas_call x1, Pallas kernels, per_device(): pl.pallas_call(functools.partial(kernel, nx, ny, n), out_shape=(field, fi...  71.8 us
    unnamed x10, local copies, waits for them, and re-layouts  5.18 us
    slice x2, local copies, waits for them, and re-layouts, per_device(): return out[:4] + (out[4][0, 0], out[5][0, 0])  2.37 us

profile of v1, /device:TPU:2, one launch (start us, length us, event | category | flops | bytes accessed | tf_op | source)
XLA Modules:
  0.0 80.0 jit_solution(8151972302679633301)
XLA Ops:
  0.6 71.8 %shard_map.145 = (f32[64,8,256]{2,1,0:T(8,128)}, f32[64,8,256]{2,1,0:T(8,128)}, f32[64,8,256]{2,1,0:T(8,128)}, f32[64,8,256]{2,1,0:T(8,128)}, f32[8,128]{1,0:T(8,128)}, /*index=5*/f32[8,128]{1,0:T(8,128)}) custom-call(f32[64,8,256]{2,1,0:T(8,128)} %des_in.1, f32[64,8,256]{2,1,0:T(8,128)} %v_in.1, f32[64,8,256]{2,1,0:T(8,128)} %t_in.1, f32[64,8,256]{2,1,0:T(8,128)} %d_in.1, ...), custom_call_target="tpu_custom_call" | custom-call | tf_op jit(solution)/shard_map/pallas_call | solution.py:738
  72.4 1.2 %slice.7 = f32[1,1]{1,0:T(1,128)} slice(f32[8,128]{1,0:T(8,128)} %get-tuple-element.17), slice={[0:1], [0:1]} | slice | bytes 8 | tf_op jit(solution)/shard_map/slice | solution.py:748
  73.6 1.2 %slice.6 = f32[1,1]{1,0:T(1,128)} slice(f32[8,128]{1,0:T(8,128)} %get-tuple-element.16), slice={[0:1], [0:1]} | slice | bytes 8 | tf_op jit(solution)/shard_map/slice | solution.py:748
  74.8 0.0 copy-start.2
  74.8 1.9 %copy.20 = f32[64,8,256]{2,1,0:T(8,128)} copy(f32[64,8,256]{2,1,0:T(8,128)} %get-tuple-element.24) | data formatting | bytes 1048576
  76.7 0.0 copy-done.2
  76.7 0.0 copy-start.1
  76.7 0.8 copy.21
  77.5 0.4 copy-done.1
  78.0 0.0 copy-start
  78.0 0.8 copy.22
  78.8 0.4 copy-done
  79.2 0.8 copy.23
Async XLA Ops:
  74.8 1.9 %copy-start.2 = (f32[64,8,256]{2,1,0:T(8,128)S(1)}, f32[64,8,256]{2,1,0:T(8,128)}, u32[]{:S(2)}) copy-start(f32[64,8,256]{2,1,0:T(8,128)} %get-tuple-element.25) | copy-start | bytes 1572868
  76.7 1.2 %copy-start.1 = (f32[64,8,256]{2,1,0:T(8,128)S(1)}, f32[64,8,256]{2,1,0:T(8,128)}, u32[]{:S(2)}) copy-start(f32[64,8,256]{2,1,0:T(8,128)} %get-tuple-element.26) | copy-start | bytes 1572868
  78.0 1.2 %copy-start = (f32[64,8,256]{2,1,0:T(8,128)S(1)}, f32[64,8,256]{2,1,0:T(8,128)}, u32[]{:S(2)}) copy-start(f32[64,8,256]{2,1,0:T(8,128)} %get-tuple-element.27) | copy-start | bytes 1572868

commit v2 on v1

--- a/solution.py
+++ b/solution.py
@@ -48,16 +48,28 @@
     return jnp.where(rows_of(p.shape) > 0, r, 0.0)
 
 
-def yz_forward(p, row):
-    q = y_next(p, row)
-    s, d = p + q, q - p
-    sz, dz = z_next(s), z_next(d)
-    return s + sz, sz - s, d + dz, dz - d
-
-
-def z_forward_rows(s, d):
-    sz, dz = z_next(s), z_next(d)
-    return s + sz, sz - s, d + dz, dz - d
+def z_forward(p):
+    q = z_next(p)
+    return p + q, q - p
+
+
+def yz_forward(p, row_s, row_d):
+    s, d = z_forward(p)
+    sy, dy = y_next(s, row_s), y_next(d, row_d)
+    return s + sy, d + dy, sy - s, dy - d
+
+
+def rows_forward(near, far):
+    (s, d), (sy, dy) = z_forward(near), z_forward(far)
+    return s + sy, d + dy, sy - s, dy - d
+
+
+def planes_after(p):
+    return pltpu.roll(p, p.shape[1] - 1, axis=1)
+
+
+def planes_before(p):
+    return pltpu.roll(p, 1, axis=1)
 
 
 def x_forward(a, b):
@@ -117,10 +129,10 @@
 def kernel(
     nx, ny, n,
     des_in, v_in, t_in, d_in, q_in, o_in, e_in, s_in, g_in, c_in,
-    v_out, t_out, d_out, f_out, occ_out, mean_out,
-    des, raw, flg, fld, flx,
+    v_out, t_out, d_out, f_out, sums_out,
+    des, raw, flg, fld, flx, zrow, coef,
     cc, cup, cdn, flo, fhi, fup, fdn,
-    wz, yf, ph, cub, cube, cubs, ca,
+    wz, yf, cub, cube, cubs, ca,
     kap, v1, v1lo, v1hi, v1up, v1dn,
     d1, d1hi, d1dn, t0, tr, t1, t1hi, t1dn, joule,
     sen, scc, sup, sdn, fil, slots1, slots2,
@@ -134,6 +146,23 @@
     first_x, last_x = gx == 0, gx == nx - 1
     first_y, last_y = gy == 0, gy == ny - 1
 
+    barrier = pltpu.get_barrier_semaphore()
+
+    def device(dx, dy):
+        return (lax.rem(gx + (nx + dx), nx), lax.rem(gy + (ny + dy), ny))
+
+    me1, block = lax.rem(gy, group), lax.div(gy, group)
+    me2 = gx * blocks + block
+
+    def peer1(k):
+        return (gx, block * group + lax.rem(me1 + k, group))
+
+    def peer2(k):
+        other = lax.rem(me2 + k, nx * blocks)
+        return (lax.div(other, blocks), lax.rem(other, blocks) * group + me1)
+
+    for dx, dy in OFFSETS:
+        pl.semaphore_signal(barrier, inc=1, device_id=device(dx, dy), device_id_type=MESH)
     loads = []
     plan = [
         (des_in, lambda h: des.at[h, PAD:end]),
@@ -162,23 +191,6 @@
             for c in loads[i]:
                 c.wait()
 
-    barrier = pltpu.get_barrier_semaphore()
-
-    def device(dx, dy):
-        return (lax.rem(gx + (nx + dx), nx), lax.rem(gy + (ny + dy), ny))
-
-    me1, block = lax.rem(gy, group), lax.div(gy, group)
-    me2 = gx * blocks + block
-
-    def peer1(k):
-        return (gx, block * group + lax.rem(me1 + k, group))
-
-    def peer2(k):
-        other = lax.rem(me2 + k, nx * blocks)
-        return (lax.div(other, blocks), lax.rem(other, blocks) * group + me1)
-
-    for dx, dy in OFFSETS:
-        pl.semaphore_signal(barrier, inc=1, device_id=device(dx, dy), device_id_type=MESH)
     for k in range(1, group):
         pl.semaphore_signal(barrier, inc=1, device_id=peer1(k), device_id_type=MESH)
     for k in range(1, nx * blocks):
@@ -238,29 +250,30 @@
 
     loaded(0)
     tails(des, cup, cdn)
+    loaded(1, 2, 3, 4, 5)
+
+    def mask_body(i, carry):
+        x = i * 8
+        free_e = flg[2, :, pl.ds(x, 8)] == 0
+        free_t = flg[3, :, pl.ds(x, 8)] == 0
+        fld[0, :, pl.ds(PAD + x, 8)] = jnp.where(free_e, raw[0, :, pl.ds(x, 8)], 0.0)
+        fld[1, :, pl.ds(PAD + x, 8)] = jnp.where(free_t, raw[1, :, pl.ds(x, 8)], 0.0)
+        fld[2, :, pl.ds(PAD + x, 8)] = jnp.where(free_t, raw[2, :, pl.ds(x, 8)], 0.0)
+        return carry
+
+    lax.fori_loop(0, n // 8, mask_body, 0)
+    for f in range(3):
+        for h in range(2):
+            fup[f, h] = row_pack(fld.at[f], h, PAD, n, 7)
+            fdn[f, h] = row_pack(fld.at[f], h, PAD, n, 0)
+    loaded(6, 7)
     pl.semaphore_wait(barrier, len(OFFSETS) + group - 1 + nx * blocks - 1)
     moving = send_up(cup, cc.at[0:3]) + send_down(cdn, cc.at[5:8])
     moving += [
         send(des.at[:, end - 4 : end], des.at[:, PAD - 4 : PAD], 1, 0),
         send(des.at[:, PAD : PAD + 3], des.at[:, end : end + 3], -1, 0),
+        send(flg.at[0:2, :, n - 1], flx, 1, 0),
     ]
-    loaded(1, 2, 3, 4, 5, 6, 7)
-    moving.append(send(flg.at[0:2, :, n - 1], flx, 1, 0))
-
-    def mask_body(i, carry):
-        x = i * 4
-        free_e = flg[2, :, pl.ds(x, 4)] == 0
-        free_t = flg[3, :, pl.ds(x, 4)] == 0
-        fld[0, :, pl.ds(PAD + x, 4)] = jnp.where(free_e, raw[0, :, pl.ds(x, 4)], 0.0)
-        fld[1, :, pl.ds(PAD + x, 4)] = jnp.where(free_t, raw[1, :, pl.ds(x, 4)], 0.0)
-        fld[2, :, pl.ds(PAD + x, 4)] = jnp.where(free_t, raw[2, :, pl.ds(x, 4)], 0.0)
-        return carry
-
-    lax.fori_loop(0, n // 4, mask_body, 0)
-    for f in range(3):
-        for h in range(2):
-            fup[f, h] = row_pack(fld.at[f], h, PAD, n, 7)
-            fdn[f, h] = row_pack(fld.at[f], h, PAD, n, 0)
     fields_moving = send_up(fup, flo) + send_down(fdn, fhi)
     fields_moving += [
         send(fld.at[:, :, end - 1 : end], fld.at[:, :, PAD - 1 : PAD], 1, 0),
@@ -269,24 +282,40 @@
 
     row = lax.broadcasted_iota(jnp.int32, (8, 128), 0)
 
-    def filter_y(ref, edge, p):
+    def filter_y(ref, p):
         for h in range(2):
             a = ref[h, p]
-            out = 4.0 * a + edge_column(edge, h, p)
+            out = 4.0 * a
             for k in (1, 2, 3):
                 out += jnp.where(row < 8 - k, float(4 - k), 0.0) * pltpu.roll(a, 8 - k, axis=0)
                 out += jnp.where(row >= k, float(4 - k), 0.0) * pltpu.roll(a, k, axis=0)
             yf[h, p] = out
 
-    def filter_y_all(ref, edge, low):
+    def filter_y_own(ref):
         def body(i, carry):
-            for u in range(4):
-                filter_y(ref, edge, PAD + 4 * i + u)
+            for u in range(8):
+                filter_y(ref, PAD + 8 * i + u)
             return carry
 
-        lax.fori_loop(0, n // 4, body, 0)
-        for p in list(range(PAD - low, PAD)) + list(range(end, end + 3)):
-            filter_y(ref, edge, p)
+        lax.fori_loop(0, n // 8, body, 0)
+
+    def filter_y_rest(ref, edge, low):
+        outer = list(range(PAD - low, PAD)) + list(range(end, end + 3))
+        for p in outer:
+            filter_y(ref, p)
+
+        def add(p):
+            for h in range(2):
+                yf[h, p] += edge_column(edge, h, p)
+
+        def body(i, carry):
+            for u in range(8):
+                add(PAD + 8 * i + u)
+            return carry
+
+        lax.fori_loop(0, n // 8, body, 0)
+        for p in outer:
+            add(p)
 
     def filter_xz(p, planes):
         halves = []
@@ -332,6 +361,7 @@
             k == 0, 1 / 10.0, jnp.where(k == 1, 1 / 13.0, jnp.where(k == 2, 1 / 15.0, r))
         ).astype(F32)
 
+    filter_y_own(des)
     arrived(moving)
 
     def clear(edge, field, low, high):
@@ -355,7 +385,7 @@
             edge[5:8] = jnp.zeros((3, 2, end + PAD, 128), F32)
 
     clear(cc, des, 4, 3)
-    filter_y_all(des, cc, 4)
+    filter_y_rest(des, cc, 4)
     there_x = jnp.where(first_x, 0.0, 1.0).astype(F32)
     there_y = jnp.where(first_y, 0.0, 1.0).astype(F32)
 
@@ -372,8 +402,10 @@
         for u in range(8):
             x = 8 * i + u
             rho = density(smoothed[:, u], p + u, flg[0, :, x], flg[1, :, x])
-            ph[:, x] = rho
-            cub[:, p + u] = rho * rho * rho
+            squared = rho * rho
+            held = (flg[0, :, x] + flg[1, :, x]) == 0
+            coef[:, x] = jnp.where(held, (3.0 * squared) * inv_yz * inv_x(p + u), 0.0)
+            cub[:, p + u] = squared * rho
             acc = acc + rho
         return acc
 
@@ -381,16 +413,16 @@
 
     for h in range(2):
         cubs[0, h] = row_pack(cub, h, 0, end, 7)
-    cube_moving = [send(cubs, cube, 0, 1)]
+    cube_moving = [send(cubs, cube.at[:, :, 0:end], 0, 1)]
 
     def gather_body(i, last):
-        for u in range(4):
-            now = spread(cub[:, PAD + 4 * i + u])
-            ca[:, 4 * i + u] = now + last
+        for u in range(8):
+            now = spread(cub[:, PAD + 8 * i + u])
+            ca[:, 8 * i + u] = now + last
             last = now
         return last
 
-    lax.fori_loop(0, n // 4, gather_body, spread(cub[:, PAD - 1]))
+    lax.fori_loop(0, n // 8, gather_body, spread(cub[:, PAD - 1]))
 
     arrived(fields_moving)
 
@@ -404,13 +436,27 @@
     def _():
         fhi[...] = jnp.zeros((3, 2, end + PAD, 128), F32)
 
+    def far_rows(k, edge):
+        s, d = z_forward(edge)
+        zrow[k, 0] = s
+        zrow[k, 1] = d
+
+    def forward_of(field, k):
+        def forward(p):
+            return yz_forward(
+                field[:, p], zrow[k, 0, :, pl.ds(p, 1)], zrow[k, 1, :, pl.ds(p, 1)]
+            )
+
+        return forward
+
+    for f in range(3):
+        far_rows(f, fhi[f])
     weights = ((0.001, 0.999), (0.05, 0.95), (0.05, 0.95))
 
     def apply_main(f):
         base, slope = weights[f]
 
-        def forward(p):
-            return yz_forward(fld[f, :, p], fhi[f, :, pl.ds(p, 1)])
+        forward = forward_of(fld.at[f], f)
 
         def element(a, b, w):
             return x_backward(*weigh(*x_forward(a, b), w))
@@ -421,50 +467,42 @@
 
         def body(i, carry):
             a, behind = carry
-            for u in range(2):
-                x = 2 * i + u
+            for u in range(8):
+                x = 8 * i + u
                 b = forward(PAD + x + 1)
                 front, new = element(a, b, base + slope * cub[:, PAD + x])
                 kap[f, :, x] = yz_backward([front[c] + behind[c] for c in range(4)])
                 a, behind = b, new
             return tuple(a), tuple(new)
 
-        lax.fori_loop(0, n // 2, body, (tuple(b), tuple(behind)))
+        lax.fori_loop(0, n // 8, body, (tuple(b), tuple(behind)))
 
     def edge_weight(base, slope):
-        where = lax.broadcasted_iota(jnp.int32, (2, end, 128), 1)
+        where = lax.broadcasted_iota(jnp.int32, (2, end + PAD, 128), 1)
         real = jnp.where(where == PAD - 1, there_x, 1.0) * there_y
         return base * real + (slope * there_y) * cube[0]
 
+    def whole_row(ref, j):
+        return jnp.stack([row_pack(ref, h, 0, end + PAD, j) for h in range(2)])
+
+    def rows_x_forward(a):
+        return x_forward(a, [planes_after(c) for c in a])
+
     def apply_edge(f):
-        low, own = flo[f, :, 0:end], fdn[f]
-        mine = jnp.concatenate([fld_first(f, PAD - 8, 8), own], axis=1)
-        s, d = mine + low, mine - low
-        a = z_forward_rows(s, d)
-        last_own = fld_first(f, end, 1)
-        last_low = flo[f, :, end : end + 1]
-        b_end = z_forward_rows(last_own + last_low, last_own - last_low)
-        where = lax.broadcasted_iota(jnp.int32, (2, end, 128), 1)
-        b = [
-            jnp.where(where == end - 1, jnp.broadcast_to(b_end[c], a[c].shape), pltpu.roll(a[c], end - 1, axis=1))
-            for c in range(4)
-        ]
-        front, behind = x_backward(*weigh(*x_forward(a, b), edge_weight(*weights[f])))
-        m = [front[c] + pltpu.roll(behind[c], 1, axis=1) for c in range(4)]
+        a = rows_forward(flo[f], whole_row(fld.at[f], 0))
+        front, behind = x_backward(*weigh(*rows_x_forward(a), edge_weight(*weights[f])))
+        m = [front[c] + planes_before(behind[c]) for c in range(4)]
         ns, nd = m[0] + m[2], m[1] + m[3]
         out = (ns - nd) + z_prev(ns + nd)
         for h in range(2):
             row_add(kap.at[f], h, 0, n, 0, out[h, PAD:end])
 
-    def fld_first(f, p, planes):
-        return jnp.stack([row_pack(fld.at[f], h, p, planes, 0) for h in range(2)])
-
     apply_main(0)
 
     arrived(cube_moving)
     apply_edge(0)
     edge_cube = cube[0] * there_y
-    edge_cube = edge_cube + pltpu.roll(edge_cube, 1, axis=1)
+    edge_cube = edge_cube + planes_before(edge_cube)
     edge_cube = edge_cube + z_prev(edge_cube)
     for h in range(2):
         row_add(ca, h, 0, n, 0, edge_cube[h, PAD:end])
@@ -476,14 +514,14 @@
     loaded(8, 9)
 
     def volt_body(i, carry):
-        for u in range(4):
-            x = 4 * i + u
+        for u in range(8):
+            x = 8 * i + u
             v = raw[0, :, x]
             moved = 1.8 * (raw[3, :, x] - kap[0, :, x]) / pivot(x, 0.001, 0.999)
             v1[:, PAD + x] = v + jnp.where(flg[2, :, x] == 0, moved, -0.6 * v)
         return carry
 
-    lax.fori_loop(0, n // 4, volt_body, 0)
+    lax.fori_loop(0, n // 8, volt_body, 0)
     for h in range(2):
         v1up[0, h] = row_pack(v1, h, PAD, n, 7)
         v1dn[0, h] = row_pack(v1, h, PAD, n, 0)
@@ -510,8 +548,8 @@
     apply_edge(1)
 
     def heat_body(i, carry):
-        for u in range(2):
-            x = 2 * i + u
+        for u in range(8):
+            x = 8 * i + u
             free = flg[3, :, x] == 0
             step = 1.8 / pivot(x, 0.05, 0.95)
             d = raw[2, :, x]
@@ -521,7 +559,7 @@
             tr[:, x] = jnp.where(free, step, 0.0)
         return carry
 
-    lax.fori_loop(0, n // 2, heat_body, 0)
+    lax.fori_loop(0, n // 8, heat_body, 0)
     for h in range(2):
         d1dn[0, h] = row_pack(d1, h, PAD, n, 0)
     dual_moving = send_down(d1dn, d1hi, both=False)
@@ -543,9 +581,8 @@
 
     clear_high(v1, v1hi, v1lo)
 
-    def volt_forward(p):
-        return yz_forward(v1[:, p], v1hi[0, :, pl.ds(p, 1)])
-
+    far_rows(3, v1hi[0])
+    volt_forward = forward_of(v1, 3)
     a = volt_forward(PAD - 1)
     b = volt_forward(PAD)
     s, d = x_forward(a, b)
@@ -553,8 +590,8 @@
 
     def joule_body(i, carry):
         a, last, acc = carry
-        for u in range(2):
-            x = 2 * i + u
+        for u in range(8):
+            x = 8 * i + u
             b = volt_forward(PAD + x + 1)
             s, d = x_forward(a, b)
             e = energy(s, d, s, d)
@@ -567,24 +604,13 @@
         return tuple(a), last, acc
 
     _, _, warm = lax.fori_loop(
-        0, n // 2, joule_body, (tuple(b), spread(lead), jnp.zeros(shape, F32))
+        0, n // 8, joule_body, (tuple(b), spread(lead), jnp.zeros(shape, F32))
     )
 
     def edge_heat():
-        low = v1lo[0, :, 0:end]
-        own = jnp.stack([row_pack(v1, h, 0, end, 0) for h in range(2)])
-        a = z_forward_rows(own + low, own - low)
-        last_own = jnp.stack([row_pack(v1, h, end, 1, 0) for h in range(2)])
-        last_low = v1lo[0, :, end : end + 1]
-        b_end = z_forward_rows(last_own + last_low, last_own - last_low)
-        where = lax.broadcasted_iota(jnp.int32, (2, end, 128), 1)
-        b = [
-            jnp.where(where == end - 1, jnp.broadcast_to(b_end[c], a[c].shape), pltpu.roll(a[c], end - 1, axis=1))
-            for c in range(4)
-        ]
-        s, d = x_forward(a, b)
+        s, d = rows_x_forward(rows_forward(v1lo[0], whole_row(v1, 0)))
         e = energy(s, d, s, d) * (edge_weight(0.001, 0.999) * 0.125)
-        e = e + pltpu.roll(e, 1, axis=1)
+        e = e + planes_before(e)
         return (e + z_prev(e))[:, PAD:end]
 
     extra = edge_heat()
@@ -601,42 +627,53 @@
     store(lambda h: t1.at[h, PAD:end], t_out)
 
     arrived(dual_moving)
-    arrived(temp_moving)
     clear_high(d1, d1hi)
-    clear_high(t1, t1hi)
+    far_rows(4, d1hi[0])
+    dual_forward = forward_of(d1, 4)
+    none = jnp.zeros((2, 1, 128), F32)
 
     def pair_forward(p):
-        return (
-            tuple(yz_forward(t1[:, p], t1hi[0, :, pl.ds(p, 1)])),
-            tuple(yz_forward(d1[:, p], d1hi[0, :, pl.ds(p, 1)])),
-        )
+        return tuple(yz_forward(t1[:, p], none, none)), tuple(dual_forward(p))
 
     def sens_body(i, carry):
         ta, da = carry
-        for u in range(2):
-            x = 2 * i + u
+        for u in range(8):
+            x = 8 * i + u
             tb, db = pair_forward(PAD + x + 1)
             ts, td = x_forward(ta, tb)
             ds, dd = x_forward(da, db)
             mean = (0.999 / 8.0) * (da[0] + db[0])
-            rho = ph[:, x]
-            raw_value = joule[:, x] * mean - 0.95 * energy(ts, td, ds, dd)
-            value = (3.0 * rho * rho) * raw_value * inv_yz * inv_x(PAD + x)
-            held = (flg[0, :, x] + flg[1, :, x]) == 0
-            sen[:, PAD + x] = jnp.where(held, value, 0.0)
+            value = joule[:, x] * mean - 0.95 * energy(ts, td, ds, dd)
+            sen[:, PAD + x] = coef[:, x] * value
             ta, da = tb, db
         return ta, da
 
-    lax.fori_loop(0, n // 2, sens_body, pair_forward(PAD))
+    carry = lax.fori_loop(0, n // 8 - 1, sens_body, pair_forward(PAD))
+    dual_s, dual_d = rows_x_forward(rows_forward(whole_row(d1, 7), d1hi[0]))
+    arrived(temp_moving)
+    clear_high(t1, t1hi)
+    sens_body(n // 8 - 1, carry)
+    behind_s, behind_d = z_forward(t1hi[0])
+    temp_s, temp_d = rows_x_forward((behind_s, behind_d, behind_s, behind_d))
+    work = 0.95 * energy(temp_s, temp_d, dual_s, dual_d)
+    for h in range(2):
+        row_add(sen, h, PAD, n, 7, -work[h, PAD:end] * row_pack(coef, h, 0, n, 7))
     tails(sen, sup, sdn)
     sens_moving = send_up(sup, scc.at[0:3]) + send_down(sdn, scc.at[5:8])
     sens_moving += [
         send(sen.at[:, end - 3 : end], sen.at[:, PAD - 3 : PAD], 1, 0),
         send(sen.at[:, PAD : PAD + 3], sen.at[:, end : end + 3], -1, 0),
     ]
+    filter_y_own(sen)
+
+    def whole(a):
+        return jnp.sum(jnp.sum(a, axis=0, keepdims=True), axis=1, keepdims=True)
+
+    occupied_sum = whole(occupied[0] + occupied[1])
+    warm_sum = whole(warm[0] + warm[1] + warm_rows)
     arrived(sens_moving)
     clear(scc, sen, 3, 3)
-    filter_y_all(sen, scc, 3)
+    filter_y_rest(sen, scc, 3)
 
     def last_body(i, acc):
         out = filter_xz(PAD + 8 * i, 8)
@@ -644,60 +681,67 @@
         return acc + jnp.sum(out * out, axis=1)
 
     square = lax.fori_loop(0, n // 8, last_body, jnp.zeros(shape, F32))
-
-    def fold(a):
-        return jnp.sum(a, axis=0, keepdims=True)
-
-    message = jnp.concatenate(
-        [
-            fold(square[0] + square[1]),
-            fold(occupied[0] + occupied[1]),
-            fold(warm[0] + warm[1] + warm_rows),
-            jnp.zeros((5, 128), F32),
-        ],
-        axis=0,
+    store(lambda h: fil.at[h], f_out)
+
+    lane = lax.broadcasted_iota(jnp.int32, (1, 128), 1)
+    message = jnp.where(
+        lane == 0,
+        whole(square[0] + square[1]),
+        jnp.where(lane == 1, occupied_sum, warm_sum),
     )
 
     def exchange(value, slots, me, size, peer, sends, recvs):
-        slots[me] = value
-        out = []
+        slots[me, 0:1] = value
         for k in range(1, size):
-            c = pltpu.make_async_remote_copy(
-                src_ref=slots.at[me], dst_ref=slots.at[me], send_sem=sends.at[k],
-                recv_sem=recvs.at[me], device_id=peer(k), device_id_type=MESH,
-            )
-            c.start()
-            out.append(c)
-        for k in range(1, size):
-            source = lax.rem(me + k, size)
             pltpu.make_async_remote_copy(
-                src_ref=slots.at[source], dst_ref=slots.at[source], send_sem=sends.at[k],
-                recv_sem=recvs.at[source], device_id=peer(k), device_id_type=MESH,
-            ).wait_recv()
-        for c in out:
-            c.wait_send()
-        result = slots[0]
-        for k in range(1, size):
-            result = result + slots[k]
-        return result
+                src_ref=slots.at[me, pl.ds(0, 1)], dst_ref=slots.at[me, pl.ds(0, 1)],
+                send_sem=sends.at[0], recv_sem=recvs.at[0],
+                device_id=peer(k), device_id_type=MESH,
+            ).start()
+        others = slots.at[pl.ds(0, size - 1), pl.ds(0, 1)]
+        every = pltpu.make_async_remote_copy(
+            src_ref=others, dst_ref=others, send_sem=sends.at[0], recv_sem=recvs.at[0],
+            device_id=peer(1), device_id_type=MESH,
+        )
+        every.wait_recv()
+        pending.append(every)
+        parts = [slots[k, 0:1] for k in range(size)]
+        while len(parts) > 1:
+            parts = [a + b for a, b in zip(parts[::2], parts[1::2])]
+        return parts[0]
 
     message = exchange(message, slots1, me1, group, peer1, r1_send, r1_recv)
     message = exchange(message, slots2, me2, nx * blocks, peer2, r2_send, r2_recv)
-    sums = jnp.sum(message, axis=1, keepdims=True)
-    scale = 1.0 / jnp.sqrt(sums[0:1] * (1.0 / total) + 1e-6)
-    scale = jnp.broadcast_to(scale, (8, 128))
-
-    def scale_body(i, carry):
-        fil[:, pl.ds(8 * i, 8)] = fil[:, pl.ds(8 * i, 8)] * scale
-        return carry
-
-    lax.fori_loop(0, n // 8, scale_body, 0)
-    store(lambda h: fil.at[h], f_out)
-    occ_out[...] = jnp.broadcast_to(sums[1:2] * (1.0 / total), (8, 128))
-    mean_out[...] = jnp.broadcast_to(sums[2:3] * (1.0 / total), (8, 128))
+    sums_out[...] = jnp.broadcast_to(message, (8, 128))
     for c in pending:
         c.wait_send()
     for c in stores:
+        c.wait()
+
+
+def finish(
+    total, v, t, d, f, sums_ref, v_out, t_out, d_out, f_out, occ_out, mean_out, buf, sem
+):
+    copies = [
+        pltpu.make_async_copy(src, dst, sem.at[i])
+        for i, (src, dst) in enumerate(((f, buf), (v, v_out), (t, t_out), (d, d_out)))
+    ]
+    for c in copies:
+        c.start()
+    sums = sums_ref[0:1] * (1.0 / total)
+    scale = jnp.broadcast_to(1.0 / jnp.sqrt(sums[:, 0:1] + 1e-6), (8, 256))
+    occ_out[0] = sums[0, 1]
+    mean_out[0] = sums[0, 2]
+    copies[0].wait()
+    parts = 4
+    step = buf.shape[0] // parts
+    for i in range(parts):
+        part = pl.ds(step * i, step)
+        buf[part] = buf[part] * scale
+        c = pltpu.make_async_copy(buf.at[part], f_out.at[part], sem.at[4 + i])
+        c.start()
+        copies.append(c)
+    for c in copies[1:]:
         c.wait()
 
 
@@ -720,32 +764,44 @@
     scratch = [
         planes, vm(5, 2, n, 8, 128), vm(4, 2, n, 8, 128, dtype=jnp.int32),
         vm(3, 2, wide, 8, 128), vm(2, 2, 8, 128, dtype=jnp.int32),
+        vm(5, 2, 2, wide, 128), own,
         vm(8, 2, wide, 128), vm(3, 2, n, 128), vm(3, 2, n, 128),
         vm(3, 2, wide, 128), vm(3, 2, wide, 128), vm(3, 2, n, 128), vm(3, 2, n, 128),
-        vm(256, 256, dtype=BF16), planes, own, planes,
-        vm(1, 2, PAD + n, 128), vm(1, 2, PAD + n, 128), own,
+        vm(256, 256, dtype=BF16), planes, planes,
+        edge, vm(1, 2, PAD + n, 128), own,
         vm(3, 2, n, 8, 128), planes, edge, edge, edge_out, edge_out,
         planes, edge, edge_out, own, own, planes, edge, edge_out, own,
         planes, vm(8, 2, wide, 128), vm(3, 2, n, 128), vm(3, 2, n, 128), own,
         vm(group, 8, 128), vm(second, 8, 128),
         pltpu.SemaphoreType.DMA((20,)), pltpu.SemaphoreType.DMA((8,)),
         pltpu.SemaphoreType.DMA((48,)), pltpu.SemaphoreType.DMA((48,)),
-        pltpu.SemaphoreType.DMA((group,)), pltpu.SemaphoreType.DMA((group,)),
-        pltpu.SemaphoreType.DMA((second,)), pltpu.SemaphoreType.DMA((second,)),
+        pltpu.SemaphoreType.DMA((1,)), pltpu.SemaphoreType.DMA((1,)),
+        pltpu.SemaphoreType.DMA((1,)), pltpu.SemaphoreType.DMA((1,)),
     ]
     anywhere = pl.BlockSpec(memory_space=pl.ANY)
+    hbm = pl.BlockSpec(memory_space=pltpu.HBM)
     vmem = pl.BlockSpec(memory_space=pltpu.VMEM)
-    out = pl.pallas_call(
+    smem = pl.BlockSpec(memory_space=pltpu.SMEM)
+    *fields, sums = pl.pallas_call(
         functools.partial(kernel, nx, ny, n),
-        out_shape=(field, field, field, field, tile, tile),
-        in_specs=[anywhere] * 10,
-        out_specs=(anywhere,) * 4 + (vmem, vmem),
+        out_shape=(field, field, field, field, tile),
+        in_specs=[hbm] * 10,
+        out_specs=(anywhere,) * 4 + (vmem,),
         scratch_shapes=scratch,
         compiler_params=pltpu.CompilerParams(
-            collective_id=0, has_side_effects=True, vmem_limit_bytes=56 * 1024 * 1024
+            collective_id=0, has_side_effects=True, vmem_limit_bytes=103 * 512 * 1024
         ),
     )(*args)
-    return out[:4] + (out[4][0, 0], out[5][0, 0])
+    one = jax.ShapeDtypeStruct((1,), F32)
+    *outs, occupied, mean = pl.pallas_call(
+        functools.partial(finish, float(nx * ny * n * 8 * 256)),
+        out_shape=(field, field, field, field, one, one),
+        in_specs=[anywhere] * 4 + [vmem],
+        out_specs=(hbm,) * 4 + (smem, smem),
+        scratch_shapes=[vm(n, 8, 256), pltpu.SemaphoreType.DMA((8,))],
+        compiler_params=pltpu.CompilerParams(vmem_limit_bytes=8 * 1024 * 1024),
+    )(*fields, sums)
+    return (*outs, occupied.reshape(()), mean.reshape(()))
 
 
 def solution(mesh):

time: 81.3 us -> 56.5 us (0.69)
  Pallas kernels: 71.8 us -> 55.2 us
  local copies, waits for them, and re-layouts: 7.56 us -> 0 us
    pallas_call x1, Pallas kernels: 71.8 us -> 53.2 us  [per_device(): pl.pallas_call(functools.partial(kernel, nx, ny, n), out_shape=(field, fi...]
    unnamed x10 -> x0, local copies, waits for them, and re-layouts: 5.18 us -> none
    slice x2 -> x0, local copies, waits for them, and re-layouts: 2.37 us -> none  [per_device(): return out[:4] + (out[4][0, 0], out[5][0, 0])]
    pallas_call x0 -> x1, Pallas kernels: none -> 1.93 us  [per_device(): pl.pallas_call(functools.partial(finish, float(nx * ny * n * 8 * 256)), o...]
where the time goes in v2:
time: 56.5 us; the launch traced here: 55.8 us
  Pallas kernels  55.2 us (98%)
  between operations  0.64 us (1%)
    pallas_call x1, Pallas kernels, per_device(): pl.pallas_call(functools.partial(kernel, nx, ny, n), out_shape=(field, fi...  53.2 us
    pallas_call x1, Pallas kernels, per_device(): pl.pallas_call(functools.partial(finish, float(nx * ny * n * 8 * 256)), o...  1.93 us

profile of v2, /device:TPU:2, one launch (start us, length us, event | category | flops | bytes accessed | tf_op | source)
XLA Modules:
  0.0 55.8 jit_solution(259690444030357504)
XLA Ops:
  0.6 53.2 %shard_map.145 = (f32[64,8,256]{2,1,0:T(8,128)S(1)}, f32[64,8,256]{2,1,0:T(8,128)S(1)}, f32[64,8,256]{2,1,0:T(8,128)S(1)}, f32[64,8,256]{2,1,0:T(8,128)S(1)}, f32[8,128]{1,0:T(8,128)S(1)}) custom-call(f32[64,8,256]{2,1,0:T(8,128)} %des_in.1, f32[64,8,256]{2,1,0:T(8,128)} %v_in.1, f32[64,8,256]{2,1,0:T(8,128)} %t_in.1, f32[64,8,256]{2,1,0:T(8,128)} %d_in.1, ...), custom_call_target="tpu_custom_call" | custom-call | tf_op jit(solution)/shard_map/pallas_call | solution.py:785
  53.9 1.9 %shard_map.146 = (f32[64,8,256]{2,1,0:T(8,128)}, f32[64,8,256]{2,1,0:T(8,128)}, f32[64,8,256]{2,1,0:T(8,128)}, f32[64,8,256]{2,1,0:T(8,128)}, f32[1]{0:T(128)}, /*index=5*/f32[1]{0:T(128)}) custom-call(f32[64,8,256]{2,1,0:T(8,128)S(1)} %get-tuple-element.17.v, f32[64,8,256]{2,1,0:T(8,128)S(1)} %get-tuple-element.18.t, ...), custom_call_target="tpu_custom_call" | custom-call | tf_op jit(solution)/shard_map/pallas_call | solution.py:796

commit v3 on v2

--- a/solution.py
+++ b/solution.py
@@ -139,8 +139,6 @@
     in_sem, out_sem, send_sem, recv_sem, r1_send, r1_recv, r2_send, r2_recv,
 ):
     gx, gy = lax.axis_index("gx"), lax.axis_index("gy")
-    group = min(16, ny)
-    blocks = ny // group
     total = float(nx * n * ny * 8 * 256)
     end = PAD + n
     first_x, last_x = gx == 0, gx == nx - 1
@@ -151,15 +149,19 @@
     def device(dx, dy):
         return (lax.rem(gx + (nx + dx), nx), lax.rem(gy + (ny + dy), ny))
 
-    me1, block = lax.rem(gy, group), lax.div(gy, group)
-    me2 = gx * blocks + block
+    chip, core = lax.div(gy, 2), lax.rem(gy, 2)
+    size1, size2 = nx * 2, ny // 2
+    me1, me2 = gx * 2 + core, chip
 
     def peer1(k):
-        return (gx, block * group + lax.rem(me1 + k, group))
+        other = lax.rem(me1 + k, size1)
+        return (lax.div(other, 2), chip * 2 + lax.rem(other, 2))
 
     def peer2(k):
-        other = lax.rem(me2 + k, nx * blocks)
-        return (lax.div(other, blocks), lax.rem(other, blocks) * group + me1)
+        return (gx, lax.rem(me2 + k, size2) * 2 + core)
+
+    def farthest_first(size):
+        return sorted(range(1, size), key=lambda k: abs(2 * k - size))
 
     for dx, dy in OFFSETS:
         pl.semaphore_signal(barrier, inc=1, device_id=device(dx, dy), device_id_type=MESH)
@@ -191,12 +193,16 @@
             for c in loads[i]:
                 c.wait()
 
-    for k in range(1, group):
+    for k in farthest_first(size1):
         pl.semaphore_signal(barrier, inc=1, device_id=peer1(k), device_id_type=MESH)
-    for k in range(1, nx * blocks):
+    for k in farthest_first(size2):
         pl.semaphore_signal(barrier, inc=1, device_id=peer2(k), device_id_type=MESH)
 
     count = [0]
+
+    def exists(dx, dy):
+        x, y = gx + dx, gy + dy
+        return (x >= 0) & (x < nx) & (y >= 0) & (y < ny)
 
     def send(src, dst, dx, dy):
         k = count[0]
@@ -205,8 +211,12 @@
             src_ref=src, dst_ref=dst, send_sem=send_sem.at[k], recv_sem=recv_sem.at[k],
             device_id=device(dx, dy), device_id_type=MESH,
         )
-        c.start()
-        return c
+
+        @pl.when(exists(dx, dy))
+        def _():
+            c.start()
+
+        return c, dx, dy
 
     def send_up(src, dst):
         return [
@@ -227,8 +237,12 @@
     pending = []
 
     def arrived(copies):
-        for c in copies:
-            c.wait_recv()
+        for c, dx, dy in copies:
+
+            @pl.when(exists(-dx, -dy))
+            def _(c=c):
+                c.wait_recv()
+
         pending.extend(copies)
 
     def tails(ref, up, down):
@@ -267,18 +281,25 @@
             fup[f, h] = row_pack(fld.at[f], h, PAD, n, 7)
             fdn[f, h] = row_pack(fld.at[f], h, PAD, n, 0)
     loaded(6, 7)
-    pl.semaphore_wait(barrier, len(OFFSETS) + group - 1 + nx * blocks - 1)
+    pl.semaphore_wait(barrier, len(OFFSETS) + size1 - 1 + size2 - 1)
     moving = send_up(cup, cc.at[0:3]) + send_down(cdn, cc.at[5:8])
     moving += [
         send(des.at[:, end - 4 : end], des.at[:, PAD - 4 : PAD], 1, 0),
         send(des.at[:, PAD : PAD + 3], des.at[:, end : end + 3], -1, 0),
         send(flg.at[0:2, :, n - 1], flx, 1, 0),
     ]
-    fields_moving = send_up(fup, flo) + send_down(fdn, fhi)
-    fields_moving += [
-        send(fld.at[:, :, end - 1 : end], fld.at[:, :, PAD - 1 : PAD], 1, 0),
-        send(fld.at[:, :, PAD : PAD + 1], fld.at[:, :, end : end + 1], -1, 0),
-    ]
+
+    def send_fields(a, b):
+        return (
+            send_up(fup.at[a:b], flo.at[a:b])
+            + send_down(fdn.at[a:b], fhi.at[a:b])
+            + [
+                send(fld.at[a:b, :, end - 1 : end], fld.at[a:b, :, PAD - 1 : PAD], 1, 0),
+                send(fld.at[a:b, :, PAD : PAD + 1], fld.at[a:b, :, end : end + 1], -1, 0),
+            ]
+        )
+
+    volt_field_moving = send_fields(0, 1)
 
     row = lax.broadcasted_iota(jnp.int32, (8, 128), 0)
 
@@ -363,6 +384,7 @@
 
     filter_y_own(des)
     arrived(moving)
+    heat_fields_moving = send_fields(1, 3)
 
     def clear(edge, field, low, high):
         @pl.when(first_x)
@@ -424,17 +446,29 @@
 
     lax.fori_loop(0, n // 8, gather_body, spread(cub[:, PAD - 1]))
 
-    arrived(fields_moving)
-
-    @pl.when(last_x)
-    def _():
-        fld[:, :, end] = jnp.zeros((3, 2, 8, 128), F32)
-        flo[:, :, end : end + PAD] = jnp.zeros((3, 2, PAD, 128), F32)
-        fhi[:, :, end : end + PAD] = jnp.zeros((3, 2, PAD, 128), F32)
-
-    @pl.when(last_y)
-    def _():
-        fhi[...] = jnp.zeros((3, 2, end + PAD, 128), F32)
+    def clear_fields(a, b):
+        @pl.when(first_x)
+        def _():
+            fld[a:b, :, PAD - 1] = jnp.zeros((b - a, 2, 8, 128), F32)
+            flo[a:b, :, 0:PAD] = jnp.zeros((b - a, 2, PAD, 128), F32)
+            fhi[a:b, :, 0:PAD] = jnp.zeros((b - a, 2, PAD, 128), F32)
+
+        @pl.when(last_x)
+        def _():
+            fld[a:b, :, end] = jnp.zeros((b - a, 2, 8, 128), F32)
+            flo[a:b, :, end : end + PAD] = jnp.zeros((b - a, 2, PAD, 128), F32)
+            fhi[a:b, :, end : end + PAD] = jnp.zeros((b - a, 2, PAD, 128), F32)
+
+        @pl.when(first_y)
+        def _():
+            flo[a:b] = jnp.zeros((b - a, 2, end + PAD, 128), F32)
+
+        @pl.when(last_y)
+        def _():
+            fhi[a:b] = jnp.zeros((b - a, 2, end + PAD, 128), F32)
+
+    arrived(volt_field_moving)
+    clear_fields(0, 1)
 
     def far_rows(k, edge):
         s, d = z_forward(edge)
@@ -449,8 +483,7 @@
 
         return forward
 
-    for f in range(3):
-        far_rows(f, fhi[f])
+    far_rows(0, fhi[0])
     weights = ((0.001, 0.999), (0.05, 0.95), (0.05, 0.95))
 
     def apply_main(f):
@@ -500,6 +533,11 @@
     apply_main(0)
 
     arrived(cube_moving)
+
+    @pl.when(first_y)
+    def _():
+        cube[0] = jnp.zeros((2, end + PAD, 128), F32)
+
     apply_edge(0)
     edge_cube = cube[0] * there_y
     edge_cube = edge_cube + planes_before(edge_cube)
@@ -542,6 +580,10 @@
 
     store(lambda h: v1.at[h, PAD:end], v_out)
 
+    arrived(heat_fields_moving)
+    clear_fields(1, 3)
+    far_rows(1, fhi[1])
+    far_rows(2, fhi[2])
     apply_main(2)
     apply_edge(2)
     apply_main(1)
@@ -580,6 +622,17 @@
             edges[0][0] = jnp.zeros((2, end + PAD, 128), F32)
 
     clear_high(v1, v1hi, v1lo)
+
+    @pl.when(first_x)
+    def _():
+        v1[:, PAD - 1] = jnp.zeros((2, 8, 128), F32)
+        v1hi[0, :, 0:PAD] = jnp.zeros((2, PAD, 128), F32)
+        v1lo[0, :, 0:PAD] = jnp.zeros((2, PAD, 128), F32)
+
+    @pl.when(first_y)
+    def _():
+        v1lo[0] = jnp.zeros((2, end + PAD, 128), F32)
+
 
     far_rows(3, v1hi[0])
     volt_forward = forward_of(v1, 3)
@@ -692,7 +745,7 @@
 
     def exchange(value, slots, me, size, peer, sends, recvs):
         slots[me, 0:1] = value
-        for k in range(1, size):
+        for k in farthest_first(size):
             pltpu.make_async_remote_copy(
                 src_ref=slots.at[me, pl.ds(0, 1)], dst_ref=slots.at[me, pl.ds(0, 1)],
                 send_sem=sends.at[0], recv_sem=recvs.at[0],
@@ -704,17 +757,21 @@
             device_id=peer(1), device_id_type=MESH,
         )
         every.wait_recv()
-        pending.append(every)
+        pending.append((every, 0, 0))
         parts = [slots[k, 0:1] for k in range(size)]
         while len(parts) > 1:
             parts = [a + b for a, b in zip(parts[::2], parts[1::2])]
         return parts[0]
 
-    message = exchange(message, slots1, me1, group, peer1, r1_send, r1_recv)
-    message = exchange(message, slots2, me2, nx * blocks, peer2, r2_send, r2_recv)
+    message = exchange(message, slots1, me1, size1, peer1, r1_send, r1_recv)
+    message = exchange(message, slots2, me2, size2, peer2, r2_send, r2_recv)
     sums_out[...] = jnp.broadcast_to(message, (8, 128))
-    for c in pending:
-        c.wait_send()
+    for c, dx, dy in pending:
+
+        @pl.when(exists(dx, dy))
+        def _(c=c):
+            c.wait_send()
+
     for c in stores:
         c.wait()
 
@@ -759,8 +816,6 @@
     own = vm(2, n, 8, 128)
     edge = vm(1, 2, wide, 128)
     edge_out = vm(1, 2, n, 128)
-    group = min(16, ny)
-    second = nx * (ny // group)
     scratch = [
         planes, vm(5, 2, n, 8, 128), vm(4, 2, n, 8, 128, dtype=jnp.int32),
         vm(3, 2, wide, 8, 128), vm(2, 2, 8, 128, dtype=jnp.int32),
@@ -772,9 +827,9 @@
         vm(3, 2, n, 8, 128), planes, edge, edge, edge_out, edge_out,
         planes, edge, edge_out, own, own, planes, edge, edge_out, own,
         planes, vm(8, 2, wide, 128), vm(3, 2, n, 128), vm(3, 2, n, 128), own,
-        vm(group, 8, 128), vm(second, 8, 128),
+        vm(nx * 2, 8, 128), vm(ny // 2, 8, 128),
         pltpu.SemaphoreType.DMA((20,)), pltpu.SemaphoreType.DMA((8,)),
-        pltpu.SemaphoreType.DMA((48,)), pltpu.SemaphoreType.DMA((48,)),
+        pltpu.SemaphoreType.DMA((64,)), pltpu.SemaphoreType.DMA((64,)),
         pltpu.SemaphoreType.DMA((1,)), pltpu.SemaphoreType.DMA((1,)),
         pltpu.SemaphoreType.DMA((1,)), pltpu.SemaphoreType.DMA((1,)),
     ]

time: 56.5 us -> 54.8 us (0.970); the launches traced: 55.8 us -> 54.7 us
  Pallas kernels: 55.2 us -> 54 us
    pallas_call x1, Pallas kernels: 53.2 us -> 52.1 us  [per_device(): pl.pallas_call(functools.partial(kernel, nx, ny, n), out_shape=(field, fi...]
where the time goes in v3:
time: 54.8 us; the launch traced here: 54.7 us
  Pallas kernels  54 us (99%)
  between operations  0.64 us (1%)
    pallas_call x1, Pallas kernels, per_device(): pl.pallas_call(functools.partial(kernel, nx, ny, n), out_shape=(field, fi...  52.1 us
    pallas_call x1, Pallas kernels, per_device(): pl.pallas_call(functools.partial(finish, float(nx * ny * n * 8 * 256)), o...  1.93 us

profile of v3, /device:TPU:2, one launch (start us, length us, event | category | flops | bytes accessed | tf_op | source)
XLA Modules:
  0.0 54.7 jit_solution(12913290244029964422)
XLA Ops:
  0.6 52.1 %shard_map.145 = (f32[64,8,256]{2,1,0:T(8,128)S(1)}, f32[64,8,256]{2,1,0:T(8,128)S(1)}, f32[64,8,256]{2,1,0:T(8,128)S(1)}, f32[64,8,256]{2,1,0:T(8,128)S(1)}, f32[8,128]{1,0:T(8,128)S(1)}) custom-call(f32[64,8,256]{2,1,0:T(8,128)} %des_in.1, f32[64,8,256]{2,1,0:T(8,128)} %v_in.1, f32[64,8,256]{2,1,0:T(8,128)} %t_in.1, f32[64,8,256]{2,1,0:T(8,128)} %d_in.1, ...), custom_call_target="tpu_custom_call" | custom-call | tf_op jit(solution)/shard_map/pallas_call | solution.py:840
  52.7 1.9 %shard_map.146 = (f32[64,8,256]{2,1,0:T(8,128)}, f32[64,8,256]{2,1,0:T(8,128)}, f32[64,8,256]{2,1,0:T(8,128)}, f32[64,8,256]{2,1,0:T(8,128)}, f32[1]{0:T(128)}, /*index=5*/f32[1]{0:T(128)}) custom-call(f32[64,8,256]{2,1,0:T(8,128)S(1)} %get-tuple-element.17.v, f32[64,8,256]{2,1,0:T(8,128)S(1)} %get-tuple-element.18.t, ...), custom_call_target="tpu_custom_call" | custom-call | tf_op jit(solution)/shard_map/pallas_call | solution.py:851

commit v4 on v3

--- a/solution.py
+++ b/solution.py
@@ -141,6 +141,7 @@
     gx, gy = lax.axis_index("gx"), lax.axis_index("gy")
     total = float(nx * n * ny * 8 * 256)
     end = PAD + n
+    big, half = min(32, n), min(16, n)
     first_x, last_x = gx == 0, gx == nx - 1
     first_y, last_y = gy == 0, gy == ny - 1
 
@@ -184,9 +185,15 @@
             c = pltpu.make_async_copy(
                 src.at[:, :, pl.ds(128 * h, 128)], dst(h), in_sem.at[2 * i + h]
             )
-            c.start()
             pair.append(c)
         loads.append(pair)
+
+    def load(*which):
+        for i in which:
+            for c in loads[i]:
+                c.start()
+
+    load(0, 1, 2)
 
     def loaded(*which):
         for i in which:
@@ -245,49 +252,42 @@
 
         pending.extend(copies)
 
-    def tails(ref, up, down):
+    def tails_up(ref, up):
         for h in range(2):
-            r = [row_pack(ref, h, PAD, n, j) for j in (0, 1, 2, 5, 6, 7)]
-            up[0, h] = r[3] + 2.0 * r[4] + 3.0 * r[5]
-            up[1, h] = r[4] + 2.0 * r[5]
-            up[2, h] = r[5]
-            down[0, h] = r[0]
-            down[1, h] = 2.0 * r[0] + r[1]
-            down[2, h] = 3.0 * r[0] + 2.0 * r[1] + r[2]
-
-    zero_rows = jnp.zeros((2, 2, end + PAD, 128), F32)
-    cc[3:5] = zero_rows
-    scc[3:5] = zero_rows
-    wi = lax.broadcasted_iota(jnp.int32, (256, 256), 0)
-    wj = lax.broadcasted_iota(jnp.int32, (256, 256), 1)
-    wz[...] = jnp.maximum(4 - jnp.abs(wi - wj), 0).astype(F32).astype(BF16)
+            a, b, c = (row_pack(ref, h, PAD, n, j) for j in (5, 6, 7))
+            up[0, h] = a + 2.0 * b + 3.0 * c
+            up[1, h] = b + 2.0 * c
+            up[2, h] = c
+
+    def tails_down(ref, down):
+        for h in range(2):
+            a, b, c = (row_pack(ref, h, PAD, n, j) for j in (0, 1, 2))
+            down[0, h] = a
+            down[1, h] = 2.0 * a + b
+            down[2, h] = 3.0 * a + 2.0 * b + c
 
     loaded(0)
-    tails(des, cup, cdn)
-    loaded(1, 2, 3, 4, 5)
-
-    def mask_body(i, carry):
-        x = i * 8
-        free_e = flg[2, :, pl.ds(x, 8)] == 0
-        free_t = flg[3, :, pl.ds(x, 8)] == 0
-        fld[0, :, pl.ds(PAD + x, 8)] = jnp.where(free_e, raw[0, :, pl.ds(x, 8)], 0.0)
-        fld[1, :, pl.ds(PAD + x, 8)] = jnp.where(free_t, raw[1, :, pl.ds(x, 8)], 0.0)
-        fld[2, :, pl.ds(PAD + x, 8)] = jnp.where(free_t, raw[2, :, pl.ds(x, 8)], 0.0)
-        return carry
-
-    lax.fori_loop(0, n // 8, mask_body, 0)
-    for f in range(3):
-        for h in range(2):
-            fup[f, h] = row_pack(fld.at[f], h, PAD, n, 7)
-            fdn[f, h] = row_pack(fld.at[f], h, PAD, n, 0)
-    loaded(6, 7)
+    load(3, 4, 5, 6, 7, 8, 9)
+    tails_down(des, cdn)
+    tails_up(des, cup)
     pl.semaphore_wait(barrier, len(OFFSETS) + size1 - 1 + size2 - 1)
     moving = send_up(cup, cc.at[0:3]) + send_down(cdn, cc.at[5:8])
     moving += [
         send(des.at[:, end - 4 : end], des.at[:, PAD - 4 : PAD], 1, 0),
         send(des.at[:, PAD : PAD + 3], des.at[:, end : end + 3], -1, 0),
-        send(flg.at[0:2, :, n - 1], flx, 1, 0),
     ]
+
+    def mask(f, flag):
+        def body(i, carry):
+            x = i * 16
+            free = flg[flag, :, pl.ds(x, 16)] == 0
+            fld[f, :, pl.ds(PAD + x, 16)] = jnp.where(free, raw[f, :, pl.ds(x, 16)], 0.0)
+            return carry
+
+        lax.fori_loop(0, n // 16, body, 0)
+        for h in range(2):
+            fup[f, h] = row_pack(fld.at[f], h, PAD, n, 7)
+            fdn[f, h] = row_pack(fld.at[f], h, PAD, n, 0)
 
     def send_fields(a, b):
         return (
@@ -299,7 +299,20 @@
             ]
         )
 
+    loaded(1, 2)
+    mask(0, 2)
     volt_field_moving = send_fields(0, 1)
+    loaded(6, 7)
+    moving.append(send(flg.at[0:2, :, n - 1], flx, 1, 0))
+    zero_rows = jnp.zeros((2, 2, end + PAD, 128), F32)
+    cc[3:5] = zero_rows
+    scc[3:5] = zero_rows
+    wi = lax.broadcasted_iota(jnp.int32, (256, 256), 0)
+    wj = lax.broadcasted_iota(jnp.int32, (256, 256), 1)
+    wz[...] = jnp.maximum(4 - jnp.abs(wi - wj), 0).astype(F32).astype(BF16)
+    loaded(3, 4, 5)
+    mask(1, 3)
+    mask(2, 3)
 
     row = lax.broadcasted_iota(jnp.int32, (8, 128), 0)
 
@@ -419,10 +432,10 @@
     cub[:, PAD - 1] = there_x * (before * before * before)
 
     def density_body(i, acc):
-        p = PAD + 8 * i
-        smoothed = filter_xz(p, 8)
-        for u in range(8):
-            x = 8 * i + u
+        p = PAD + big * i
+        smoothed = filter_xz(p, big)
+        for u in range(big):
+            x = big * i + u
             rho = density(smoothed[:, u], p + u, flg[0, :, x], flg[1, :, x])
             squared = rho * rho
             held = (flg[0, :, x] + flg[1, :, x]) == 0
@@ -431,7 +444,7 @@
             acc = acc + rho
         return acc
 
-    occupied = lax.fori_loop(0, n // 8, density_body, jnp.zeros(shape, F32))
+    occupied = lax.fori_loop(0, n // big, density_body, jnp.zeros(shape, F32))
 
     for h in range(2):
         cubs[0, h] = row_pack(cub, h, 0, end, 7)
@@ -486,29 +499,32 @@
     far_rows(0, fhi[0])
     weights = ((0.001, 0.999), (0.05, 0.95), (0.05, 0.95))
 
-    def apply_main(f):
-        base, slope = weights[f]
-
-        forward = forward_of(fld.at[f], f)
+    def apply_main(which, base, slope, step):
+        forwards = [forward_of(fld.at[f], f) for f in which]
 
         def element(a, b, w):
             return x_backward(*weigh(*x_forward(a, b), w))
 
-        a = forward(PAD - 1)
-        b = forward(PAD)
-        _, behind = element(a, b, there_x * base + slope * cub[:, PAD - 1])
+        start = []
+        w = there_x * base + slope * cub[:, PAD - 1]
+        for forward in forwards:
+            a, b = forward(PAD - 1), forward(PAD)
+            start.append((tuple(b), tuple(element(a, b, w)[1])))
 
         def body(i, carry):
-            a, behind = carry
-            for u in range(8):
-                x = 8 * i + u
-                b = forward(PAD + x + 1)
-                front, new = element(a, b, base + slope * cub[:, PAD + x])
-                kap[f, :, x] = yz_backward([front[c] + behind[c] for c in range(4)])
-                a, behind = b, new
-            return tuple(a), tuple(new)
-
-        lax.fori_loop(0, n // 8, body, (tuple(b), tuple(behind)))
+            carry = list(carry)
+            for u in range(step):
+                x = step * i + u
+                w = base + slope * cub[:, PAD + x]
+                for k, f in enumerate(which):
+                    a, behind = carry[k]
+                    b = forwards[k](PAD + x + 1)
+                    front, new = element(a, b, w)
+                    kap[f, :, x] = yz_backward([front[c] + behind[c] for c in range(4)])
+                    carry[k] = tuple(b), tuple(new)
+            return tuple(carry)
+
+        lax.fori_loop(0, n // step, body, tuple(start))
 
     def edge_weight(base, slope):
         where = lax.broadcasted_iota(jnp.int32, (2, end + PAD, 128), 1)
@@ -530,7 +546,7 @@
         for h in range(2):
             row_add(kap.at[f], h, 0, n, 0, out[h, PAD:end])
 
-    apply_main(0)
+    apply_main((0,), *weights[0], big)
 
     arrived(cube_moving)
 
@@ -584,10 +600,9 @@
     clear_fields(1, 3)
     far_rows(1, fhi[1])
     far_rows(2, fhi[2])
-    apply_main(2)
+    apply_main((1, 2), *weights[1], half)
+    apply_edge(1)
     apply_edge(2)
-    apply_main(1)
-    apply_edge(1)
 
     def heat_body(i, carry):
         for u in range(8):
@@ -636,6 +651,23 @@
 
     far_rows(3, v1hi[0])
     volt_forward = forward_of(v1, 3)
+    def row_energy(near, far):
+        s, d = rows_x_forward(rows_forward(near, far))
+        return energy(s, d, s, d)
+
+    def row_gather(e):
+        e = e + planes_before(e)
+        return (e + z_prev(e))[:, PAD:end]
+
+    row0 = whole_row(v1, 0)
+    extra = row_gather(row_energy(v1lo[0], row0) * (edge_weight(0.001, 0.999) * 0.125))
+    where = lax.broadcasted_iota(jnp.int32, (2, end + PAD, 128), 1)
+    own_weight = 0.001 * jnp.where(where == PAD - 1, there_x, 1.0) + 0.999 * whole_row(cub, 0)
+    heat0 = extra + row_gather(row_energy(row0, whole_row(v1, 1)) * (own_weight * 0.125))
+    for h in range(2):
+        t1dn[0, h] = row_pack(t0, h, 0, n, 0) + row_pack(tr, h, 0, n, 0) * heat0[h]
+    temp_moving = send_down(t1dn, t1hi, both=False)
+
     a = volt_forward(PAD - 1)
     b = volt_forward(PAD)
     s, d = x_forward(a, b)
@@ -643,8 +675,8 @@
 
     def joule_body(i, carry):
         a, last, acc = carry
-        for u in range(8):
-            x = 8 * i + u
+        for u in range(half):
+            x = half * i + u
             b = volt_forward(PAD + x + 1)
             s, d = x_forward(a, b)
             e = energy(s, d, s, d)
@@ -656,27 +688,19 @@
             a, last = b, now
         return tuple(a), last, acc
 
-    _, _, warm = lax.fori_loop(
-        0, n // 8, joule_body, (tuple(b), spread(lead), jnp.zeros(shape, F32))
-    )
-
-    def edge_heat():
-        s, d = rows_x_forward(rows_forward(v1lo[0], whole_row(v1, 0)))
-        e = energy(s, d, s, d) * (edge_weight(0.001, 0.999) * 0.125)
-        e = e + planes_before(e)
-        return (e + z_prev(e))[:, PAD:end]
-
-    extra = edge_heat()
+    carry = joule_body(0, (tuple(b), spread(lead), jnp.zeros(shape, F32)))
+    for h in range(2):
+        t1[h, PAD, 0:1] += extra[h, 0:1] * tr[h, 0, 0:1]
+    temp_moving.append(send(t1.at[:, PAD : PAD + 1], t1.at[:, end : end + 1], -1, 0))
+    _, _, warm = lax.fori_loop(1, n // half, joule_body, carry)
+
     warm_rows = jnp.zeros((8, 128), F32)
     for h in range(2):
         more = extra[h] * row_pack(tr, h, 0, n, 0)
-        row_add(t1, h, PAD, n, 0, more)
+        row_add(t1, h, PAD + 1, n - 1, 0, more[1:])
         warm_rows = warm_rows + jnp.sum(
             (more * row_pack(raw.at[4], h, 0, n, 0)).reshape(n // 8, 8, 128), axis=0
         )
-        t1dn[0, h] = row_pack(t1, h, PAD, n, 0)
-    temp_moving = send_down(t1dn, t1hi, both=False)
-    temp_moving.append(send(t1.at[:, PAD : PAD + 1], t1.at[:, end : end + 1], -1, 0))
     store(lambda h: t1.at[h, PAD:end], t_out)
 
     arrived(dual_moving)
@@ -690,8 +714,8 @@
 
     def sens_body(i, carry):
         ta, da = carry
-        for u in range(8):
-            x = 8 * i + u
+        for u in range(half):
+            x = half * i + u
             tb, db = pair_forward(PAD + x + 1)
             ts, td = x_forward(ta, tb)
             ds, dd = x_forward(da, db)
@@ -701,18 +725,20 @@
             ta, da = tb, db
         return ta, da
 
-    carry = lax.fori_loop(0, n // 8 - 1, sens_body, pair_forward(PAD))
+    carry = lax.fori_loop(0, n // half - 1, sens_body, pair_forward(PAD))
     dual_s, dual_d = rows_x_forward(rows_forward(whole_row(d1, 7), d1hi[0]))
     arrived(temp_moving)
     clear_high(t1, t1hi)
-    sens_body(n // 8 - 1, carry)
+    sens_body(n // half - 1, carry)
+    tails_down(sen, sdn)
+    sens_moving = send_down(sdn, scc.at[5:8])
     behind_s, behind_d = z_forward(t1hi[0])
     temp_s, temp_d = rows_x_forward((behind_s, behind_d, behind_s, behind_d))
     work = 0.95 * energy(temp_s, temp_d, dual_s, dual_d)
     for h in range(2):
         row_add(sen, h, PAD, n, 7, -work[h, PAD:end] * row_pack(coef, h, 0, n, 7))
-    tails(sen, sup, sdn)
-    sens_moving = send_up(sup, scc.at[0:3]) + send_down(sdn, scc.at[5:8])
+    tails_up(sen, sup)
+    sens_moving += send_up(sup, scc.at[0:3])
     sens_moving += [
         send(sen.at[:, end - 3 : end], sen.at[:, PAD - 3 : PAD], 1, 0),
         send(sen.at[:, PAD : PAD + 3], sen.at[:, end : end + 3], -1, 0),
@@ -729,11 +755,11 @@
     filter_y_rest(sen, scc, 3)
 
     def last_body(i, acc):
-        out = filter_xz(PAD + 8 * i, 8)
-        fil[:, pl.ds(8 * i, 8)] = out
+        out = filter_xz(PAD + big * i, big)
+        fil[:, pl.ds(big * i, big)] = out
         return acc + jnp.sum(out * out, axis=1)
 
-    square = lax.fori_loop(0, n // 8, last_body, jnp.zeros(shape, F32))
+    square = lax.fori_loop(0, n // big, last_body, jnp.zeros(shape, F32))
     store(lambda h: fil.at[h], f_out)
 
     lane = lax.broadcasted_iota(jnp.int32, (1, 128), 1)

time: 54.8 us -> 50.2 us (0.916)
  Pallas kernels: 54 us -> 49.5 us
    pallas_call x1, Pallas kernels: 52.1 us -> 47.5 us  [per_device(): pl.pallas_call(functools.partial(kernel, nx, ny, n), out_shape=(field, fi...]
where the time goes in v4:
time: 50.2 us; the launch traced here: 50.1 us
  Pallas kernels  49.5 us (99%)
  between operations  0.64 us (1%)
    pallas_call x1, Pallas kernels, per_device(): pl.pallas_call(functools.partial(kernel, nx, ny, n), out_shape=(field, fi...  47.5 us
    pallas_call x1, Pallas kernels, per_device(): pl.pallas_call(functools.partial(finish, float(nx * ny * n * 8 * 256)), o...  1.93 us

profile of v4, /device:TPU:2, one launch (start us, length us, event | category | flops | bytes accessed | tf_op | source)
XLA Modules:
  0.0 50.1 jit_solution(7146448260177290229)
XLA Ops:
  0.6 47.5 %shard_map.145 = (f32[64,8,256]{2,1,0:T(8,128)S(1)}, f32[64,8,256]{2,1,0:T(8,128)S(1)}, f32[64,8,256]{2,1,0:T(8,128)S(1)}, f32[64,8,256]{2,1,0:T(8,128)S(1)}, f32[8,128]{1,0:T(8,128)S(1)}) custom-call(f32[64,8,256]{2,1,0:T(8,128)} %des_in.1, f32[64,8,256]{2,1,0:T(8,128)} %v_in.1, f32[64,8,256]{2,1,0:T(8,128)} %t_in.1, f32[64,8,256]{2,1,0:T(8,128)} %d_in.1, ...), custom_call_target="tpu_custom_call" | custom-call | tf_op jit(solution)/shard_map/pallas_call | solution.py:866
  48.2 1.9 %shard_map.146 = (f32[64,8,256]{2,1,0:T(8,128)}, f32[64,8,256]{2,1,0:T(8,128)}, f32[64,8,256]{2,1,0:T(8,128)}, f32[64,8,256]{2,1,0:T(8,128)}, f32[1]{0:T(128)}, /*index=5*/f32[1]{0:T(128)}) custom-call(f32[64,8,256]{2,1,0:T(8,128)S(1)} %get-tuple-element.17.v, f32[64,8,256]{2,1,0:T(8,128)S(1)} %get-tuple-element.18.t, ...), custom_call_target="tpu_custom_call" | custom-call | tf_op jit(solution)/shard_map/pallas_call | solution.py:877

commit v5 on v4

--- a/solution.py
+++ b/solution.py
@@ -164,8 +164,6 @@
     def farthest_first(size):
         return sorted(range(1, size), key=lambda k: abs(2 * k - size))
 
-    for dx, dy in OFFSETS:
-        pl.semaphore_signal(barrier, inc=1, device_id=device(dx, dy), device_id_type=MESH)
     loads = []
     plan = [
         (des_in, lambda h: des.at[h, PAD:end]),
@@ -193,17 +191,22 @@
             for c in loads[i]:
                 c.start()
 
-    load(0, 1, 2)
+    load(0)
 
     def loaded(*which):
         for i in which:
             for c in loads[i]:
                 c.wait()
 
-    for k in farthest_first(size1):
-        pl.semaphore_signal(barrier, inc=1, device_id=peer1(k), device_id_type=MESH)
-    for k in farthest_first(size2):
-        pl.semaphore_signal(barrier, inc=1, device_id=peer2(k), device_id_type=MESH)
+    for k in range(max(size1, size2) - 1):
+        for size, peer in ((size2, peer2), (size1, peer1)):
+            if k < size - 1:
+                pl.semaphore_signal(
+                    barrier, inc=1, device_id=peer(farthest_first(size)[k]), device_id_type=MESH
+                )
+    for dx, dy in OFFSETS:
+        pl.semaphore_signal(barrier, inc=1, device_id=device(dx, dy), device_id_type=MESH)
+    load(1, 2)
 
     count = [0]
 
@@ -807,24 +810,23 @@
 ):
     copies = [
         pltpu.make_async_copy(src, dst, sem.at[i])
-        for i, (src, dst) in enumerate(((f, buf), (v, v_out), (t, t_out), (d, d_out)))
+        for i, (src, dst) in enumerate(((v, v_out), (t, t_out), (d, d_out)))
     ]
     for c in copies:
         c.start()
     sums = sums_ref[0:1] * (1.0 / total)
     scale = jnp.broadcast_to(1.0 / jnp.sqrt(sums[:, 0:1] + 1e-6), (8, 256))
-    occ_out[0] = sums[0, 1]
-    mean_out[0] = sums[0, 2]
-    copies[0].wait()
     parts = 4
     step = buf.shape[0] // parts
     for i in range(parts):
         part = pl.ds(step * i, step)
-        buf[part] = buf[part] * scale
-        c = pltpu.make_async_copy(buf.at[part], f_out.at[part], sem.at[4 + i])
+        buf[part] = f[part] * scale
+        c = pltpu.make_async_copy(buf.at[part], f_out.at[part], sem.at[3 + i])
         c.start()
         copies.append(c)
-    for c in copies[1:]:
+    occ_out[0] = sums[0, 1]
+    mean_out[0] = sums[0, 2]
+    for c in copies:
         c.wait()
 
 
@@ -877,7 +879,7 @@
     *outs, occupied, mean = pl.pallas_call(
         functools.partial(finish, float(nx * ny * n * 8 * 256)),
         out_shape=(field, field, field, field, one, one),
-        in_specs=[anywhere] * 4 + [vmem],
+        in_specs=[anywhere] * 3 + [vmem, vmem],
         out_specs=(hbm,) * 4 + (smem, smem),
         scratch_shapes=[vm(n, 8, 256), pltpu.SemaphoreType.DMA((8,))],
         compiler_params=pltpu.CompilerParams(vmem_limit_bytes=8 * 1024 * 1024),

time: 50.2 us -> 50 us (level)
  no operation moved by 1% of the time
where the time goes in v5:
time: 50 us; the launch traced here: 49.9 us
  Pallas kernels  49.3 us (99%)
  between operations  0.64 us (1%)
    pallas_call x1, Pallas kernels, per_device(): pl.pallas_call(functools.partial(kernel, nx, ny, n), out_shape=(field, fi...  47.4 us
    pallas_call x1, Pallas kernels, per_device(): pl.pallas_call(functools.partial(finish, float(nx * ny * n * 8 * 256)), o...  1.9 us

profile of v5, /device:TPU:2, one launch (start us, length us, event | category | flops | bytes accessed | tf_op | source)
XLA Modules:
  0.0 49.9 jit_solution(3175320483395927181)
XLA Ops:
  0.6 47.4 %shard_map.145 = (f32[64,8,256]{2,1,0:T(8,128)S(1)}, f32[64,8,256]{2,1,0:T(8,128)S(1)}, f32[64,8,256]{2,1,0:T(8,128)S(1)}, f32[64,8,256]{2,1,0:T(8,128)S(1)}, f32[8,128]{1,0:T(8,128)S(1)}) custom-call(f32[64,8,256]{2,1,0:T(8,128)} %des_in.1, f32[64,8,256]{2,1,0:T(8,128)} %v_in.1, f32[64,8,256]{2,1,0:T(8,128)} %t_in.1, f32[64,8,256]{2,1,0:T(8,128)} %d_in.1, ...), custom_call_target="tpu_custom_call" | custom-call | tf_op jit(solution)/shard_map/pallas_call | solution.py:868
  48.0 1.9 %shard_map.146 = (f32[64,8,256]{2,1,0:T(8,128)}, f32[64,8,256]{2,1,0:T(8,128)}, f32[64,8,256]{2,1,0:T(8,128)}, f32[64,8,256]{2,1,0:T(8,128)}, f32[1]{0:T(128)}, /*index=5*/f32[1]{0:T(128)}) custom-call(f32[64,8,256]{2,1,0:T(8,128)S(1)} %get-tuple-element.17.v, f32[64,8,256]{2,1,0:T(8,128)S(1)} %get-tuple-element.18.t, ...), custom_call_target="tpu_custom_call" | custom-call | tf_op jit(solution)/shard_map/pallas_call | solution.py:879

commit v6 on v5

--- a/solution.py
+++ b/solution.py
@@ -141,7 +141,8 @@
     gx, gy = lax.axis_index("gx"), lax.axis_index("gy")
     total = float(nx * n * ny * 8 * 256)
     end = PAD + n
-    big, half = min(32, n), min(16, n)
+    big, half = min(32, n // 2), min(16, n)
+    split = big + 8
     first_x, last_x = gx == 0, gx == nx - 1
     first_y, last_y = gy == 0, gy == ny - 1
 
@@ -244,6 +245,18 @@
             some.append(send(src.at[:, :, n - PAD : n], dst.at[:, :, 0:PAD], 1, -1))
         return some
 
+    def send_first(src, dst, dy):
+        return [
+            send(src.at[:, :, 0:split], dst.at[:, :, PAD : PAD + split], 0, dy),
+            send(src.at[:, :, n - PAD : n], dst.at[:, :, 0:PAD], 1, dy),
+        ]
+
+    def send_second(src, dst, dy):
+        return [
+            send(src.at[:, :, split:n], dst.at[:, :, PAD + split : end], 0, dy),
+            send(src.at[:, :, 0:PAD], dst.at[:, :, end : end + PAD], -1, dy),
+        ]
+
     pending = []
 
     def arrived(copies):
@@ -274,11 +287,10 @@
     tails_down(des, cdn)
     tails_up(des, cup)
     pl.semaphore_wait(barrier, len(OFFSETS) + size1 - 1 + size2 - 1)
-    moving = send_up(cup, cc.at[0:3]) + send_down(cdn, cc.at[5:8])
-    moving += [
-        send(des.at[:, end - 4 : end], des.at[:, PAD - 4 : PAD], 1, 0),
-        send(des.at[:, PAD : PAD + 3], des.at[:, end : end + 3], -1, 0),
-    ]
+    moving1 = send_first(cup, cc.at[0:3], 1) + send_first(cdn, cc.at[5:8], -1)
+    moving1.append(send(des.at[:, end - 4 : end], des.at[:, PAD - 4 : PAD], 1, 0))
+    moving2 = send_second(cup, cc.at[0:3], 1) + send_second(cdn, cc.at[5:8], -1)
+    moving2.append(send(des.at[:, PAD : PAD + 3], des.at[:, end : end + 3], -1, 0))
 
     def mask(f, flag):
         def body(i, carry):
@@ -306,7 +318,7 @@
     mask(0, 2)
     volt_field_moving = send_fields(0, 1)
     loaded(6, 7)
-    moving.append(send(flg.at[0:2, :, n - 1], flx, 1, 0))
+    moving2.append(send(flg.at[0:2, :, n - 1], flx, 1, 0))
     zero_rows = jnp.zeros((2, 2, end + PAD, 128), F32)
     cc[3:5] = zero_rows
     scc[3:5] = zero_rows
@@ -336,8 +348,7 @@
 
         lax.fori_loop(0, n // 8, body, 0)
 
-    def filter_y_rest(ref, edge, low):
-        outer = list(range(PAD - low, PAD)) + list(range(end, end + 3))
+    def filter_y_rest(ref, edge, outer, start, stop):
         for p in outer:
             filter_y(ref, p)
 
@@ -347,12 +358,18 @@
 
         def body(i, carry):
             for u in range(8):
-                add(PAD + 8 * i + u)
+                add(start + 8 * i + u)
             return carry
 
-        lax.fori_loop(0, n // 8, body, 0)
+        lax.fori_loop(0, (stop - start) // 8, body, 0)
         for p in outer:
             add(p)
+
+    def filter_y_first(ref, edge, low):
+        filter_y_rest(ref, edge, range(PAD - low, PAD), PAD, PAD + split)
+
+    def filter_y_second(ref, edge):
+        filter_y_rest(ref, edge, range(end, end + 3), PAD + split, end)
 
     def filter_xz(p, planes):
         halves = []
@@ -399,8 +416,6 @@
         ).astype(F32)
 
     filter_y_own(des)
-    arrived(moving)
-    heat_fields_moving = send_fields(1, 3)
 
     def clear(edge, field, low, high):
         @pl.when(first_x)
@@ -423,16 +438,16 @@
             edge[5:8] = jnp.zeros((3, 2, end + PAD, 128), F32)
 
     clear(cc, des, 4, 3)
-    filter_y_rest(des, cc, 4)
+    clear(scc, sen, 3, 3)
+    arrived(moving1)
+    heat_fields_moving = send_fields(1, 3)
+    filter_y_first(des, cc, 4)
     there_x = jnp.where(first_x, 0.0, 1.0).astype(F32)
     there_y = jnp.where(first_y, 0.0, 1.0).astype(F32)
 
     def density(smoothed, p, e, s):
         solid = smoothed * inv_yz * inv_x(p)
         return jnp.where(e == 1, 0.0, jnp.where(s == 1, 1.0, solid))
-
-    before = density(filter_xz(PAD - 2, 2)[:, 1], PAD - 1, flx[0], flx[1])
-    cub[:, PAD - 1] = there_x * (before * before * before)
 
     def density_body(i, acc):
         p = PAD + big * i
@@ -447,7 +462,12 @@
             acc = acc + rho
         return acc
 
-    occupied = lax.fori_loop(0, n // big, density_body, jnp.zeros(shape, F32))
+    occupied = density_body(0, jnp.zeros(shape, F32))
+    arrived(moving2)
+    filter_y_second(des, cc)
+    occupied = lax.fori_loop(1, n // big, density_body, occupied)
+    before = density(filter_xz(PAD - 2, 2)[:, 1], PAD - 1, flx[0], flx[1])
+    cub[:, PAD - 1] = there_x * (before * before * before)
 
     for h in range(2):
         cubs[0, h] = row_pack(cub, h, 0, end, 7)
@@ -734,18 +754,18 @@
     clear_high(t1, t1hi)
     sens_body(n // half - 1, carry)
     tails_down(sen, sdn)
-    sens_moving = send_down(sdn, scc.at[5:8])
+    sens1 = send_first(sdn, scc.at[5:8], -1)
+    sens2 = send_second(sdn, scc.at[5:8], -1)
     behind_s, behind_d = z_forward(t1hi[0])
     temp_s, temp_d = rows_x_forward((behind_s, behind_d, behind_s, behind_d))
     work = 0.95 * energy(temp_s, temp_d, dual_s, dual_d)
     for h in range(2):
         row_add(sen, h, PAD, n, 7, -work[h, PAD:end] * row_pack(coef, h, 0, n, 7))
     tails_up(sen, sup)
-    sens_moving += send_up(sup, scc.at[0:3])
-    sens_moving += [
-        send(sen.at[:, end - 3 : end], sen.at[:, PAD - 3 : PAD], 1, 0),
-        send(sen.at[:, PAD : PAD + 3], sen.at[:, end : end + 3], -1, 0),
-    ]
+    sens1 += send_first(sup, scc.at[0:3], 1)
+    sens1.append(send(sen.at[:, end - 3 : end], sen.at[:, PAD - 3 : PAD], 1, 0))
+    sens2 += send_second(sup, scc.at[0:3], 1)
+    sens2.append(send(sen.at[:, PAD : PAD + 3], sen.at[:, end : end + 3], -1, 0))
     filter_y_own(sen)
 
     def whole(a):
@@ -753,16 +773,18 @@
 
     occupied_sum = whole(occupied[0] + occupied[1])
     warm_sum = whole(warm[0] + warm[1] + warm_rows)
-    arrived(sens_moving)
-    clear(scc, sen, 3, 3)
-    filter_y_rest(sen, scc, 3)
+    arrived(sens1)
+    filter_y_first(sen, scc, 3)
 
     def last_body(i, acc):
         out = filter_xz(PAD + big * i, big)
         fil[:, pl.ds(big * i, big)] = out
         return acc + jnp.sum(out * out, axis=1)
 
-    square = lax.fori_loop(0, n // big, last_body, jnp.zeros(shape, F32))
+    square = last_body(0, jnp.zeros(shape, F32))
+    arrived(sens2)
+    filter_y_second(sen, scc)
+    square = lax.fori_loop(1, n // big, last_body, square)
     store(lambda h: fil.at[h], f_out)
 
     lane = lax.broadcasted_iota(jnp.int32, (1, 128), 1)

time: 50 us -> 48.7 us (0.974)
  Pallas kernels: 49.3 us -> 47.9 us
    pallas_call x1, Pallas kernels: 47.4 us -> 46 us  [per_device(): pl.pallas_call(functools.partial(kernel, nx, ny, n), out_shape=(field, fi...]
where the time goes in v6:
time: 48.7 us; the launch traced here: 48.6 us
  Pallas kernels  47.9 us (98%)
  between operations  0.64 us (1%)
    pallas_call x1, Pallas kernels, per_device(): pl.pallas_call(functools.partial(kernel, nx, ny, n), out_shape=(field, fi...  46 us
    pallas_call x1, Pallas kernels, per_device(): pl.pallas_call(functools.partial(finish, float(nx * ny * n * 8 * 256)), o...  1.9 us

profile of v6, /device:TPU:2, one launch (start us, length us, event | category | flops | bytes accessed | tf_op | source)
XLA Modules:
  0.0 48.6 jit_solution(13797818432982955046)
XLA Ops:
  0.6 46.0 %shard_map.145 = (f32[64,8,256]{2,1,0:T(8,128)S(1)}, f32[64,8,256]{2,1,0:T(8,128)S(1)}, f32[64,8,256]{2,1,0:T(8,128)S(1)}, f32[64,8,256]{2,1,0:T(8,128)S(1)}, f32[8,128]{1,0:T(8,128)S(1)}) custom-call(f32[64,8,256]{2,1,0:T(8,128)} %des_in.1, f32[64,8,256]{2,1,0:T(8,128)} %v_in.1, f32[64,8,256]{2,1,0:T(8,128)} %t_in.1, f32[64,8,256]{2,1,0:T(8,128)} %d_in.1, ...), custom_call_target="tpu_custom_call" | custom-call | tf_op jit(solution)/shard_map/pallas_call | solution.py:890
  46.7 1.9 %shard_map.146 = (f32[64,8,256]{2,1,0:T(8,128)}, f32[64,8,256]{2,1,0:T(8,128)}, f32[64,8,256]{2,1,0:T(8,128)}, f32[64,8,256]{2,1,0:T(8,128)}, f32[1]{0:T(128)}, /*index=5*/f32[1]{0:T(128)}) custom-call(f32[64,8,256]{2,1,0:T(8,128)S(1)} %get-tuple-element.17.v, f32[64,8,256]{2,1,0:T(8,128)S(1)} %get-tuple-element.18.t, ...), custom_call_target="tpu_custom_call" | custom-call | tf_op jit(solution)/shard_map/pallas_call | solution.py:901

commit v7 on v6

--- a/solution.py
+++ b/solution.py
@@ -318,7 +318,7 @@
     mask(0, 2)
     volt_field_moving = send_fields(0, 1)
     loaded(6, 7)
-    moving2.append(send(flg.at[0:2, :, n - 1], flx, 1, 0))
+    flags_moving = [send(flg.at[0:2, :, n - 1], flx, 1, 0)]
     zero_rows = jnp.zeros((2, 2, end + PAD, 128), F32)
     cc[3:5] = zero_rows
     scc[3:5] = zero_rows
@@ -356,13 +356,7 @@
             for h in range(2):
                 yf[h, p] += edge_column(edge, h, p)
 
-        def body(i, carry):
-            for u in range(8):
-                add(start + 8 * i + u)
-            return carry
-
-        lax.fori_loop(0, (stop - start) // 8, body, 0)
-        for p in outer:
+        for p in [*outer, *range(start, stop)]:
             add(p)
 
     def filter_y_first(ref, edge, low):
@@ -463,11 +457,12 @@
         return acc
 
     occupied = density_body(0, jnp.zeros(shape, F32))
+    arrived(flags_moving)
+    before = density(filter_xz(PAD - 2, 2)[:, 1], PAD - 1, flx[0], flx[1])
+    cub[:, PAD - 1] = there_x * (before * before * before)
     arrived(moving2)
     filter_y_second(des, cc)
     occupied = lax.fori_loop(1, n // big, density_body, occupied)
-    before = density(filter_xz(PAD - 2, 2)[:, 1], PAD - 1, flx[0], flx[1])
-    cub[:, PAD - 1] = there_x * (before * before * before)
 
     for h in range(2):
         cubs[0, h] = row_pack(cub, h, 0, end, 7)
@@ -560,9 +555,11 @@
     def rows_x_forward(a):
         return x_forward(a, [planes_after(c) for c in a])
 
-    def apply_edge(f):
-        a = rows_forward(flo[f], whole_row(fld.at[f], 0))
-        front, behind = x_backward(*weigh(*rows_x_forward(a), edge_weight(*weights[f])))
+    def edge_forward(f):
+        return rows_x_forward(rows_forward(flo[f], whole_row(fld.at[f], 0)))
+
+    def apply_edge(f, parts):
+        front, behind = x_backward(*weigh(*parts, edge_weight(*weights[f])))
         m = [front[c] + planes_before(behind[c]) for c in range(4)]
         ns, nd = m[0] + m[2], m[1] + m[3]
         out = (ns - nd) + z_prev(ns + nd)
@@ -571,13 +568,14 @@
 
     apply_main((0,), *weights[0], big)
 
+    volt_parts = edge_forward(0)
     arrived(cube_moving)
 
     @pl.when(first_y)
     def _():
         cube[0] = jnp.zeros((2, end + PAD, 128), F32)
 
-    apply_edge(0)
+    apply_edge(0, volt_parts)
     edge_cube = cube[0] * there_y
     edge_cube = edge_cube + planes_before(edge_cube)
     edge_cube = edge_cube + z_prev(edge_cube)
@@ -624,8 +622,8 @@
     far_rows(1, fhi[1])
     far_rows(2, fhi[2])
     apply_main((1, 2), *weights[1], half)
-    apply_edge(1)
-    apply_edge(2)
+    apply_edge(1, edge_forward(1))
+    apply_edge(2, edge_forward(2))
 
     def heat_body(i, carry):
         for u in range(8):
@@ -698,8 +696,8 @@
 
     def joule_body(i, carry):
         a, last, acc = carry
-        for u in range(half):
-            x = half * i + u
+        for u in range(big):
+            x = big * i + u
             b = volt_forward(PAD + x + 1)
             s, d = x_forward(a, b)
             e = energy(s, d, s, d)
@@ -715,7 +713,7 @@
     for h in range(2):
         t1[h, PAD, 0:1] += extra[h, 0:1] * tr[h, 0, 0:1]
     temp_moving.append(send(t1.at[:, PAD : PAD + 1], t1.at[:, end : end + 1], -1, 0))
-    _, _, warm = lax.fori_loop(1, n // half, joule_body, carry)
+    _, _, warm = lax.fori_loop(1, n // big, joule_body, carry)
 
     warm_rows = jnp.zeros((8, 128), F32)
     for h in range(2):

time: 48.7 us -> 48.4 us (level)
  no operation moved by 1% of the time
where the time goes in v7:
time: 48.4 us; the launch traced here: 48.3 us
  Pallas kernels  47.7 us (99%)
  between operations  0.64 us (1%)
    pallas_call x1, Pallas kernels, per_device(): pl.pallas_call(functools.partial(kernel, nx, ny, n), out_shape=(field, fi...  45.8 us
    pallas_call x1, Pallas kernels, per_device(): pl.pallas_call(functools.partial(finish, float(nx * ny * n * 8 * 256)), o...  1.9 us

profile of v7, /device:TPU:2, one launch (start us, length us, event | category | flops | bytes accessed | tf_op | source)
XLA Modules:
  0.0 48.3 jit_solution(10915095710833803446)
XLA Ops:
  0.6 45.8 %shard_map.145 = (f32[64,8,256]{2,1,0:T(8,128)S(1)}, f32[64,8,256]{2,1,0:T(8,128)S(1)}, f32[64,8,256]{2,1,0:T(8,128)S(1)}, f32[64,8,256]{2,1,0:T(8,128)S(1)}, f32[8,128]{1,0:T(8,128)S(1)}) custom-call(f32[64,8,256]{2,1,0:T(8,128)} %des_in.1, f32[64,8,256]{2,1,0:T(8,128)} %v_in.1, f32[64,8,256]{2,1,0:T(8,128)} %t_in.1, f32[64,8,256]{2,1,0:T(8,128)} %d_in.1, ...), custom_call_target="tpu_custom_call" | custom-call | tf_op jit(solution)/shard_map/pallas_call | solution.py:888
  46.4 1.9 %shard_map.146 = (f32[64,8,256]{2,1,0:T(8,128)}, f32[64,8,256]{2,1,0:T(8,128)}, f32[64,8,256]{2,1,0:T(8,128)}, f32[64,8,256]{2,1,0:T(8,128)}, f32[1]{0:T(128)}, /*index=5*/f32[1]{0:T(128)}) custom-call(f32[64,8,256]{2,1,0:T(8,128)S(1)} %get-tuple-element.17.v, f32[64,8,256]{2,1,0:T(8,128)S(1)} %get-tuple-element.18.t, ...), custom_call_target="tpu_custom_call" | custom-call | tf_op jit(solution)/shard_map/pallas_call | solution.py:899

commit v8 on v7

--- a/solution.py
+++ b/solution.py
@@ -460,13 +460,19 @@
     arrived(flags_moving)
     before = density(filter_xz(PAD - 2, 2)[:, 1], PAD - 1, flx[0], flx[1])
     cub[:, PAD - 1] = there_x * (before * before * before)
+
+    def send_cube(start, stop):
+        for h in range(2):
+            cubs[0, h, start:stop] = row_pack(cub, h, start, stop - start, 7)
+        part = (slice(None), slice(None), slice(start, stop))
+        return send(cubs.at[part], cube.at[part], 0, 1)
+
+    cube_moving = [send_cube(0, PAD + big)]
     arrived(moving2)
     filter_y_second(des, cc)
     occupied = lax.fori_loop(1, n // big, density_body, occupied)
 
-    for h in range(2):
-        cubs[0, h] = row_pack(cub, h, 0, end, 7)
-    cube_moving = [send(cubs, cube.at[:, :, 0:end], 0, 1)]
+    cube_moving.append(send_cube(PAD + big, end))
 
     def gather_body(i, last):
         for u in range(8):

time: 48.4 us -> 48.4 us (level)
  no operation moved by 1% of the time
where the time goes in v8:
time: 48.4 us; the launch traced here: 48.3 us
  Pallas kernels  47.7 us (99%)
  between operations  0.64 us (1%)
    pallas_call x1, Pallas kernels, per_device(): pl.pallas_call(functools.partial(kernel, nx, ny, n), out_shape=(field, fi...  45.8 us
    pallas_call x1, Pallas kernels, per_device(): pl.pallas_call(functools.partial(finish, float(nx * ny * n * 8 * 256)), o...  1.9 us

profile of v8, /device:TPU:2, one launch (start us, length us, event | category | flops | bytes accessed | tf_op | source)
XLA Modules:
  0.0 48.3 jit_solution(8602888365590122865)
XLA Ops:
  0.6 45.8 %shard_map.145 = (f32[64,8,256]{2,1,0:T(8,128)S(1)}, f32[64,8,256]{2,1,0:T(8,128)S(1)}, f32[64,8,256]{2,1,0:T(8,128)S(1)}, f32[64,8,256]{2,1,0:T(8,128)S(1)}, f32[8,128]{1,0:T(8,128)S(1)}) custom-call(f32[64,8,256]{2,1,0:T(8,128)} %des_in.1, f32[64,8,256]{2,1,0:T(8,128)} %v_in.1, f32[64,8,256]{2,1,0:T(8,128)} %t_in.1, f32[64,8,256]{2,1,0:T(8,128)} %d_in.1, ...), custom_call_target="tpu_custom_call" | custom-call | tf_op jit(solution)/shard_map/pallas_call | solution.py:894
  46.4 1.9 %shard_map.146 = (f32[64,8,256]{2,1,0:T(8,128)}, f32[64,8,256]{2,1,0:T(8,128)}, f32[64,8,256]{2,1,0:T(8,128)}, f32[64,8,256]{2,1,0:T(8,128)}, f32[1]{0:T(128)}, /*index=5*/f32[1]{0:T(128)}) custom-call(f32[64,8,256]{2,1,0:T(8,128)S(1)} %get-tuple-element.17.v, f32[64,8,256]{2,1,0:T(8,128)S(1)} %get-tuple-element.18.t, ...), custom_call_target="tpu_custom_call" | custom-call | tf_op jit(solution)/shard_map/pallas_call | solution.py:905
